TPU v7x, 32 devices: a whole 2x2x4 slice. The times are simulated.
32 devices in a mesh: mode: 8 (over z, y), space: 4 (over x, core).
Axes of the slice: x: 2, y: 2, z: 4, core: 2. Of those that a mesh axis runs over, the one named last changes fastest.
Arguments:
- pressure: float32 [512, 8, 4, 128], P('mode', 'space'), may hold values from -6 to 6
- source: float32 [512, 8, 4, 128], P('mode', 'space'), may hold values from -6 to 6
- coefficients: float32 [32, 8, 4, 128], P(None, 'space'), may hold values from 0.2 to 2
- coupling: float32 [32, 512, 512], P(None, 'mode'), as said below
Outputs:
- pressure_out: float32 [512, 8, 4, 128], P('mode', 'space')
- residual: float32 [512, 8, 4, 128], P('mode', 'space')
Inputs may be any that keep to these rules, and one draw needn't show every extreme that they name: coupling[k] is symmetric for every k.
All inputs are finite; a program needn't handle non-finite values.
Results may differ from a plain program's by a relative error of at most 0.00011.
Values sent between devices are 32-bit elements; how exact they have to be, the bound alone decides.
No kernel may reach another device: no remote copies, remote signals or barrier semaphores. Data moves between devices by JAX's collectives and lax.ppermute only.
A program may use at most 64 MiB of HBM per device.

v0:
```python
import jax
import jax.numpy as jnp
from jax import lax
from jax.experimental import pallas as pl
from jax.experimental.pallas import tpu as pltpu
from jax.sharding import PartitionSpec as P

ITERS = 2
LANES = 128
KINDS = 6

storage_coef = 1.0
damping = 0.7

VMEM = pl.BlockSpec(memory_space=pltpu.VMEM)
SMEM = pl.BlockSpec(memory_space=pltpu.SMEM)


def parts_of(x):
    hi = x.astype(jnp.bfloat16)
    return hi, (x - hi.astype(jnp.float32)).astype(jnp.bfloat16)


def place(u_ref, blocks, offsets):
    part = u_ref.shape[0] // 3
    for s, block in enumerate(blocks):
        rows = block.shape[0]
        hi, lo = parts_of(block[...])
        row = pl.multiple_of(offsets[s], rows)
        u_ref[pl.ds(row, rows), :] = hi
        u_ref[pl.ds(row + part, rows), :] = lo
        u_ref[pl.ds(row + 2 * part, rows), :] = hi


def lane_shift(x, offset):
    moved = pltpu.roll(x, (-offset) % LANES, 1)
    lane = lax.broadcasted_iota(jnp.int32, x.shape, 1)
    edge = 0 if offset < 0 else LANES - 1
    return jnp.where(lane == edge, 0.0, moved)


def mix_kernel(planes, half, count, odd, offsets, *refs):
    blocks, refs = refs[:count], refs[count:]
    c_ref, w_ref, press, source, part_ref, odd_ref, even_ref, field_ref, u_ref, cs_ref, sems = refs
    rows, lanes_all = press.shape
    cells = lanes_all // planes
    terms = w_ref.shape[1]
    chunk = terms // sems.shape[0]

    copies = [
        pltpu.make_async_copy(
            c_ref.at[pl.ds(k, chunk), half], cs_ref.at[pl.ds(k, chunk)], sems.at[k // chunk]
        )
        for k in range(0, terms, chunk)
    ]
    for copy in copies:
        copy.start()
    place(u_ref, blocks, offsets)
    tile = 2 * LANES if cells % (2 * LANES) == 0 else LANES

    def product(k, t):
        hi, lo = parts_of(cs_ref[k : k + chunk].reshape(chunk * rows, cs_ref.shape[2]))
        return jnp.dot(
            jnp.concatenate([hi, hi, lo], axis=1),
            u_ref[:, t * tile : (t + 1) * tile],
            preferred_element_type=jnp.float32,
        )

    def weigh(start, t, m):
        for r in range(tile // LANES):
            lanes = slice(t * tile + r * LANES, t * tile + (r + 1) * LANES)
            total = [None if start == 0 else field_ref[n, :, lanes] for n in range(KINDS)]
            for k in range(chunk):
                value = m[k * rows : (k + 1) * rows, r * LANES : (r + 1) * LANES]
                for n in range(KINDS):
                    term = w_ref[n, start + k : start + k + 1, lanes] * value
                    total[n] = term if total[n] is None else total[n] + term
            for n in range(KINDS):
                field_ref[n, :, lanes] = total[n]

    before = None
    for k in range(0, terms, chunk):
        copies[k // chunk].wait()
        for t in range(lanes_all // tile):
            m = product(k, t)
            if before is not None:
                weigh(*before)
            before = (k, t, m)
    weigh(*before)

    count = cells // LANES
    for p in range(planes):
        for r in range(count):

            def field(n, p=p, r=r):
                return field_ref[n, :, p * cells + r * LANES : p * cells + (r + 1) * LANES]

            lanes = slice(p * cells + r * LANES, p * cells + (r + 1) * LANES)
            flux = field(0) + field(1) + field(2) + field(3)
            if p > 0:
                flux = flux - field(1, p - 1, r)
            if p < planes - 1:
                flux = flux - field(0, p + 1, r)
            if r > 0:
                flux = flux - field(3, p, r - 1)
            if r < count - 1:
                flux = flux - field(2, p, r + 1)
            below, above = field(4), field(5)
            flux = flux + (below - lane_shift(above, -1)) + (above - lane_shift(below, 1))
            part_ref[:, lanes] = source[:, lanes] - storage_coef * press[:, lanes] - flux

    lower, upper = slice(0, cells), slice((planes - 1) * cells, planes * cells)
    is_odd = odd[0] == 1
    for at, (low, high) in enumerate(
        [(part_ref[:, lower], part_ref[:, upper]), (field_ref[0, :, lower], field_ref[1, :, upper])]
    ):
        odd_ref[at] = jnp.where(is_odd, high, low)
        even_ref[at] = jnp.where(is_odd, low, high)


def mix(odd, offsets, blocks, c, w, press, source, half, planes):
    rows, lanes_all = press.shape
    cells = lanes_all // planes
    terms, _, _, modes = c.shape
    chunks = max(1, terms * rows // 256)
    sent = jax.ShapeDtypeStruct((2, rows, cells), jnp.float32)
    return pl.pallas_call(
        lambda *refs: mix_kernel(planes, half, len(blocks), *refs),
        in_specs=[SMEM] * 2 + [VMEM] * len(blocks) + [pl.BlockSpec(memory_space=pltpu.HBM)] + [VMEM] * 3,
        out_specs=[VMEM] * 3,
        out_shape=[jax.ShapeDtypeStruct(press.shape, jnp.float32), sent, sent],
        scratch_shapes=[
            pltpu.VMEM((KINDS, rows, lanes_all), jnp.float32),
            pltpu.VMEM((3 * modes, lanes_all), jnp.bfloat16),
            pltpu.VMEM((terms, rows, modes), jnp.float32),
            pltpu.SemaphoreType.DMA((chunks,)),
        ],
        compiler_params=pltpu.CompilerParams(vmem_limit_bytes=20 * 2**20),
        cost_estimate=pl.CostEstimate(
            flops=6 * terms * rows * modes * lanes_all, bytes_accessed=4 * terms * rows * modes, transcendentals=0
        ),
    )(odd, offsets, *blocks, c, w, press, source)


def smooth_kernel(planes, halves, final, odd, *refs):
    w_ref, inv_ref = refs[6 * halves : 6 * halves + 2]
    outs = refs[6 * halves + 2 :]
    is_odd = odd[0] == 1
    for h in range(halves):
        part, press, odd_own, even_own, odd_in, even_in = refs[6 * h : 6 * h + 6]
        rows, lanes_all = press.shape
        cells = lanes_all // planes
        count = cells // LANES

        def lanes(p, r):
            return slice(p * cells + r * LANES, p * cells + (r + 1) * LANES)

        res, first = {}, {}
        for r in range(count):
            row = slice(r * LANES, (r + 1) * LANES)
            for p in range(planes):
                res[p, r] = part[:, lanes(p, r)]
            res[0, r] = res[0, r] + jnp.where(is_odd, even_in[1, :, row], odd_in[1, :, row])
            res[planes - 1, r] = res[planes - 1, r] + jnp.where(is_odd, odd_in[1, :, row], even_in[1, :, row])
            odd_side = odd_in[0, :, row] + odd_own[1, :, row]
            even_side = even_in[0, :, row] + even_own[1, :, row]
            res[-1, r] = jnp.where(is_odd, even_side, odd_side)
            res[planes, r] = jnp.where(is_odd, odd_side, even_side)
            for p in range(-1, planes + 1):
                first[p, r] = inv_ref[p + 1 : p + 2, row] * res[p, r]
        for p in range(planes):
            for r in range(count):
                f = first[p, r]
                row = slice(r * LANES, (r + 1) * LANES)

                def w(n):
                    return w_ref[n : n + 1, lanes(p, r)]

                mean = storage_coef * f + w(0) * (f - first[p - 1, r]) + w(1) * (f - first[p + 1, r])
                mean = mean + w(2) * (f - first[p, r - 1] if r > 0 else f)
                mean = mean + w(3) * (f - first[p, r + 1] if r < count - 1 else f)
                mean = mean + w(4) * (f - lane_shift(f, -1)) + w(5) * (f - lane_shift(f, 1))
                second = f + inv_ref[p + 1 : p + 2, row] * (res[p, r] - mean)
                new = press[:, lanes(p, r)] + second
                if final:
                    outs[0][h * rows : (h + 1) * rows, p * count + r, :] = new
                    outs[1][h * rows : (h + 1) * rows, p * count + r, :] = res[p, r]
                else:
                    outs[h][:, lanes(p, r)] = new


def smooth(odd, states, w0, inv, final):
    halves = len(states)
    rows, lanes_all = states[0][1].shape
    planes = inv.shape[0] - 2
    if final:
        out_shape = [jax.ShapeDtypeStruct((halves * rows, lanes_all // LANES, LANES), jnp.float32)] * 2
    else:
        out_shape = [jax.ShapeDtypeStruct((rows, lanes_all), jnp.float32)] * halves
    return pl.pallas_call(
        lambda *refs: smooth_kernel(planes, halves, final, *refs),
        in_specs=[SMEM] + [VMEM] * (6 * halves + 2),
        out_specs=[VMEM] * len(out_shape),
        out_shape=out_shape,
        compiler_params=pltpu.CompilerParams(vmem_limit_bytes=8 * 2**20),
        cost_estimate=pl.CostEstimate(flops=40 * halves * rows * lanes_all, bytes_accessed=0, transcendentals=0),
    )(odd, *[x for state in states for x in state], w0, inv)


def weights_kernel(beside, coef_ref, low_ref, high_ref, w_ref, w0_ref, inv_ref):
    terms = coef_ref.shape[0]
    rows = low_ref.shape[1]
    planes = coef_ref.shape[1] // rows
    a = {(p, r): coef_ref[:, p * rows + r, :] for p in range(planes) for r in range(rows)}
    a.update({(-1, r): low_ref[0:terms, r, :] for r in range(rows)})
    a.update({(planes, r): high_ref[0:terms, r, :] for r in range(rows)})
    beyond = {(-2, r): low_ref[terms : terms + 1, r, :] for r in range(rows)}
    beyond.update({(planes + 1, r): high_ref[terms : terms + 1, r, :] for r in range(rows)})

    def near(x, p, r):
        zero = jnp.zeros_like(x)
        count = x.shape[0]

        def at(q, t):
            if t < 0 or t >= rows:
                return zero
            return beyond[q, t] if (q, t) in beyond else a[q, t][0:count]

        return [at(p - 1, r), at(p + 1, r), at(p, r - 1), at(p, r + 1), lane_shift(x, -1), lane_shift(x, 1)]

    for p in range(-1, planes + 1):
        for r in range(rows):
            inside = 0 <= p < planes
            x = a[p, r] if inside else a[p, r][0:1]
            lanes = slice(p * rows * LANES + r * LANES, p * rows * LANES + (r + 1) * LANES)
            total = storage_coef
            for n, other in enumerate(near(x, p, r)):
                edge = 0.5 * (x + other)
                if inside:
                    w_ref[n, :, lanes] = edge
                    w0_ref[n : n + 1, lanes] = edge[0:1]
                total = total + edge[0:1]
            value = damping / total
            if not inside:
                value = jnp.where(beside[0 if p < 0 else 1] == 1, value, 0.0)
            inv_ref[p + 1 : p + 2, r * LANES : (r + 1) * LANES] = value


def all_weights(beside, coef, low, high):
    terms, planes, cy, cz = coef.shape
    cells = cy * cz
    return pl.pallas_call(
        weights_kernel,
        in_specs=[SMEM] + [VMEM] * 3,
        out_specs=[VMEM] * 3,
        out_shape=[
            jax.ShapeDtypeStruct((KINDS, terms, planes * cells), jnp.float32),
            jax.ShapeDtypeStruct((KINDS, planes * cells), jnp.float32),
            jax.ShapeDtypeStruct((planes + 2, cells), jnp.float32),
        ],
        compiler_params=pltpu.CompilerParams(vmem_limit_bytes=6 * 2**20),
        cost_estimate=pl.CostEstimate(flops=30 * coef.size, bytes_accessed=0, transcendentals=0),
    )(beside, coef.reshape(terms, planes * cy, cz), low, high)


def after(x, *others):
    others = [o for o in others if o is not None]
    return lax.optimization_barrier((x, *others))[0] if others else x


def gathered(halves, inner, outer):
    size = inner * outer
    ring = [(i, (i + inner) % size) for i in range(size)]
    turned = [(i, i // inner * inner + (i % inner + 1) % inner) for i in range(size)]
    found = []
    current = list(halves)
    for step in range(outer):
        sent = list(current)
        for h, block in enumerate(sent):
            found.append((block, step, 0, h))
            for turn in range(1, inner):
                block = lax.ppermute(block, "mode", turned)
                found.append((block, step, turn, h))
            if step < outer - 1:
                current[h] = after(lax.ppermute(sent[h], "mode", ring), block)
    return found


def on_device(pressure, source, coefficients, coupling):
    size, slabs = lax.axis_size("mode"), lax.axis_size("space")
    own, planes, cy, cz = pressure.shape
    cells = cy * cz
    terms = coefficients.shape[0]
    inner = max(1, LANES // own)
    outer = size // inner
    halves = 2 if own % 32 == 0 else 1
    rows = own // halves

    flat = pressure.reshape(own, planes * cells)
    press = [flat[h * rows : (h + 1) * rows] for h in range(halves)]
    found = gathered(press, inner, outer)
    mode_at = lax.axis_index("mode")
    outer_at, inner_at = mode_at // inner, mode_at % inner
    offsets = jnp.stack(
        [
            ((outer_at - f[1] + outer) % outer * inner + (inner_at - f[2] + inner) % inner) * own + f[3] * rows
            for f in found
        ]
    ).astype(jnp.int32)
    c = coupling.reshape(terms, halves, rows, size * own)

    coefficients = after(coefficients, found[inner - 1][0])
    source = after(source, found[2 * inner * halves][0])

    up = [(i, i + 1) for i in range(slabs - 1)]
    down = [(j, i) for i, j in up]
    low = lax.ppermute(jnp.concatenate([coefficients[:, planes - 1], coefficients[:1, planes - 2]]), "space", up)
    high = lax.ppermute(jnp.concatenate([coefficients[:, 0], coefficients[:1, 1]]), "space", down)
    slab = lax.axis_index("space")
    beside = jnp.stack([slab > 0, slab < slabs - 1]).astype(jnp.int32)
    w, w0, inv = all_weights(beside, coefficients, low, high)

    odd = (slab % 2).astype(jnp.int32).reshape(1)
    pairs = [[(i, i + 1) for i in range(start, slabs - 1, 2)] for start in (1, 0)]
    swap_odd, swap_even = [p + [(j, i) for i, j in p] for p in pairs]

    flat = source.reshape(own, planes * cells)
    src = [flat[h * rows : (h + 1) * rows] for h in range(halves)]
    for step in range(ITERS):
        blocks = [f[0] for f in found]
        states = []
        for h in range(halves):
            part, odd_own, even_own = mix(odd, offsets, blocks, c, w, press[h], src[h], h, planes)
            even_in = lax.ppermute(even_own, "space", swap_even)
            odd_in = lax.ppermute(odd_own, "space", swap_odd)
            states.append((part, press[h], odd_own, even_own, odd_in, even_in))
        if step < ITERS - 1:
            press = [smooth(odd, [state], w0, inv, False)[0] for state in states]
            found = gathered(press, inner, outer)
        else:
            outs = smooth(odd, states, w0, inv, True)
    return tuple(x.reshape(pressure.shape) for x in outs)


def solution(mesh):
    in_specs = (
        P("mode", "space", None, None),
        P("mode", "space", None, None),
        P(None, "space", None, None),
        P(None, "mode", None),
    )
    out_specs = (P("mode", "space", None, None), P("mode", "space", None, None))
    return jax.shard_map(
        on_device, mesh=mesh, in_specs=in_specs, out_specs=out_specs, check_vma=False
    )
```

profile of v0, /device:TPU:1, one launch (start us, length us, event | category | flops | bytes accessed | tf_op | source)
XLA Modules:
  0.0 115.2 jit_solution(5388773108438295096)
XLA Ops:
  0.6 1.0 fusion.1
  1.7 2.2 %collective-permute-start.2 = (f32[32,1024]{1,0:T(8,128)S(1)}, f32[32,1024]{1,0:T(8,128)S(1)}, u32[]{:S(2)}, u32[]{:S(2)}) collective-permute-start(f32[32,1024]{1,0:T(8,128)S(1)} %slice.37.refs_2_.refs_20_), channel_id=1, source_target_pairs={{0,8},{4,12},{8,16},{12,20},{16,24},{20,28},{24,0},{28,4},{1,9},{5... | collective-permute-start | bytes 393224 | tf_op jit(solution)/shard_map/ppermute | solution.py:285
  3.9 1.2 %collective-permute-start = (f32[32,1024]{1,0:T(8,128)S(1)}, f32[32,1024]{1,0:T(8,128)S(1)}, u32[]{:S(2)}, u32[]{:S(2)}) collective-permute-start(f32[32,1024]{1,0:T(8,128)S(1)} %slice.37.refs_2_.refs_20_), channel_id=1, source_target_pairs={{0,4},{4,0},{8,12},{12,8},{16,20},{20,16},{24,28},{28,24},{1,5},{5... | collective-permute-start | bytes 393224 | tf_op jit(solution)/shard_map/ppermute | solution.py:282
  5.2 1.3 %collective-permute-start.4 = (f32[32,1024]{1,0:T(8,128)S(1)}, f32[32,1024]{1,0:T(8,128)S(1)}, u32[]{:S(2)}, u32[]{:S(2)}) collective-permute-start(f32[32,1024]{1,0:T(8,128)S(1)} %slice.39.refs_4_.refs_20_.refs_2_), channel_id=1, source_target_pairs={{0,8},{4,12},{8,16},{12,20},{16,24},{20,28},{24,0},{28,4},{1,9},{5... | collective-permute-start | bytes 393224 | tf_op jit(solution)/shard_map/ppermute | solution.py:285
  6.5 0.2 collective-permute-start.1
  6.7 0.1 stack.76.refs_1_
  6.8 2.3 %collective-permute-done.2.refs_6_ = f32[32,1024]{1,0:T(8,128)S(1)} collective-permute-done((f32[32,1024]{1,0:T(8,128)S(1)}, f32[32,1024]{1,0:T(8,128)S(1)}, u32[]{:S(2)}, u32[]{:S(2)}) %collective-permute-start.2) | collective-permute-done | bytes 131104 | tf_op jit(solution)/shard_map/ppermute | solution.py:285
  9.1 0.2 collective-permute-start.6
  9.3 1.2 %collective-permute-start.3 = (f32[32,1024]{1,0:T(8,128)S(1)}, f32[32,1024]{1,0:T(8,128)S(1)}, u32[]{:S(2)}, u32[]{:S(2)}) collective-permute-start(f32[32,1024]{1,0:T(8,128)S(1)} %collective-permute-done.2.refs_6_), channel_id=1, source_target_pairs={{0,4},{4,0},{8,12},{12,8},{16,20},{20,16},{24,28},{28,24},{1,5},{5... | collective-permute-start | bytes 393224 | tf_op jit(solution)/shard_map/ppermute | solution.py:282
  10.5 0.5 collective-permute-done.4.refs_8_
  11.1 1.0 collective-permute-start.8
  12.1 1.5 %collective-permute-start.5 = (f32[32,1024]{1,0:T(8,128)S(1)}, f32[32,1024]{1,0:T(8,128)S(1)}, u32[]{:S(2)}, u32[]{:S(2)}) collective-permute-start(f32[32,1024]{1,0:T(8,128)S(1)} %collective-permute-done.4.refs_8_), channel_id=1, source_target_pairs={{0,4},{4,0},{8,12},{12,8},{16,20},{20,16},{24,28},{28,24},{1,5},{5... | collective-permute-start | bytes 393224 | tf_op jit(solution)/shard_map/ppermute | solution.py:282
  13.5 0.9 slice_bitcast_fusion
  14.4 0.7 slice_bitcast_fusion.2
  15.2 5.8 %collective-permute-start.14 = (f32[33,4,128]{2,1,0:T(4,128)S(1)}, f32[33,4,128]{2,1,0:T(4,128)S(1)}, u32[]{:S(2)}, u32[]{:S(2)}) collective-permute-start(f32[33,4,128]{2,1,0:T(4,128)S(1)} %pad_maximum_fusion), channel_id=1, source_target_pairs={{0,1},{1,2},{2,3},{4,5},{5,6},{6,7},{8,9},{9,10},{10,11},{12,13},{... | collective-permute-start | bytes 202760 | tf_op jit(solution)/shard_map/ppermute | solution.py:317
  21.0 1.8 %collective-permute-start.10 = (f32[32,1024]{1,0:T(8,128)S(1)}, f32[32,1024]{1,0:T(8,128)S(1)}, u32[]{:S(2)}, u32[]{:S(2)}) collective-permute-start(f32[32,1024]{1,0:T(8,128)S(1)} %collective-permute-done.6.refs_10_), channel_id=1, source_target_pairs={{0,8},{4,12},{8,16},{12,20},{16,24},{20,28},{24,0},{28,4},{1,9},{5... | collective-permute-start | bytes 393224 | tf_op jit(solution)/shard_map/ppermute | solution.py:285
  22.9 0.2 collective-permute-start.7
  23.1 0.7 collective-permute-start.12
  23.8 0.6 collective-permute-start.9
  24.4 1.9 %collective-permute-start.15 = (f32[33,4,128]{2,1,0:T(4,128)S(1)}, f32[33,4,128]{2,1,0:T(4,128)S(1)}, u32[]{:S(2)}, u32[]{:S(2)}) collective-permute-start(f32[33,4,128]{2,1,0:T(4,128)S(1)} %pad_maximum_fusion.1), channel_id=1, source_target_pairs={{1,0},{2,1},{3,2},{5,4},{6,5},{7,6},{9,8},{10,9},{11,10},{13,12},{... | collective-permute-start | bytes 202760 | tf_op jit(solution)/shard_map/ppermute | solution.py:318
  26.4 0.1 add_convert_fusion.beside
  26.4 3.6 %collective-permute-done.15.high_ref = f32[33,4,128]{2,1,0:T(4,128)S(1)} collective-permute-done((f32[33,4,128]{2,1,0:T(4,128)S(1)}, f32[33,4,128]{2,1,0:T(4,128)S(1)}, u32[]{:S(2)}, u32[]{:S(2)}) %collective-permute-start.15) | collective-permute-done | bytes 67616 | tf_op jit(solution)/shard_map/ppermute | solution.py:318
  30.0 0.9 copy-done
  30.9 1.0 shard_map.59
  32.0 0.9 collective-permute-start.11
  32.9 0.6 collective-permute-start.13
  33.5 1.0 fusion
  34.6 2.1 %collective-permute-done.11.refs_15_ = f32[32,1024]{1,0:T(8,128)S(1)} collective-permute-done((f32[32,1024]{1,0:T(8,128)S(1)}, f32[32,1024]{1,0:T(8,128)S(1)}, u32[]{:S(2)}, u32[]{:S(2)}) %collective-permute-start.11) | collective-permute-done | bytes 131104 | tf_op jit(solution)/shard_map/ppermute | solution.py:282
  36.7 1.4 %collective-permute-done.13.refs_17_ = f32[32,1024]{1,0:T(8,128)S(1)} collective-permute-done((f32[32,1024]{1,0:T(8,128)S(1)}, f32[32,1024]{1,0:T(8,128)S(1)}, u32[]{:S(2)}, u32[]{:S(2)}) %collective-permute-start.13) | collective-permute-done | bytes 131104 | tf_op jit(solution)/shard_map/ppermute | solution.py:282
  38.1 2.2 %copy-done.1 = f32[32,64,512]{2,1,0:T(8,128)S(1)} copy-done((f32[32,64,512]{2,1,0:T(8,128)S(1)}, f32[32,64,512]{2,1,0:T(8,128)}, u32[]{:S(2)}) %copy-start.1) | copy-done | bytes 4194328
  40.3 6.7 %shard_map.62 = (f32[32,1024]{1,0:T(8,128)S(1)}, f32[2,32,512]{2,1,0:T(8,128)S(1)}, f32[2,32,512]{2,1,0:T(8,128)S(1)}) custom-call(s32[1]{0:T(128)} %bitcast.refs_0_, s32[16]{0:T(128)S(1)} %stack.76.refs_1_, f32[32,1024]{1,0:T(8,128)S(1)} %slice.37.refs_2_.refs_20_, f32[32,1024]{1,0:T(8,128)S(1)} %collective-permute-done.refs_3_, ...), custom_call_target="tpu_custom_call" | custom-call | flops 3221225472 | bytes 2097152 | tf_op jit(solution)/shard_map/pallas_call | solution.py:127
  47.0 3.4 %collective-permute-start.19 = (f32[2,32,512]{2,1,0:T(8,128)S(1)}, f32[2,32,512]{2,1,0:T(8,128)S(1)}, u32[]{:S(2)}, u32[]{:S(2)}) collective-permute-start(f32[2,32,512]{2,1,0:T(8,128)S(1)} %get-tuple-element.48.refs_3_), channel_id=1, source_target_pairs={{1,2},{2,1},{5,6},{6,5},{9,10},{10,9},{13,14},{14,13},{17,18},{18,... | collective-permute-start | bytes 393224 | tf_op jit(solution)/shard_map/ppermute | solution.py:335
  50.4 0.1 collective-permute-start.20
  50.5 6.7 %shard_map.60 = (f32[32,1024]{1,0:T(8,128)S(1)}, f32[2,32,512]{2,1,0:T(8,128)S(1)}, f32[2,32,512]{2,1,0:T(8,128)S(1)}) custom-call(s32[1]{0:T(128)} %bitcast.refs_0_, s32[16]{0:T(128)S(1)} %stack.76.refs_1_, f32[32,1024]{1,0:T(8,128)S(1)} %slice.37.refs_2_.refs_20_, f32[32,1024]{1,0:T(8,128)S(1)} %collective-permute-done.refs_3_, ...), custom_call_target="tpu_custom_call" | custom-call | flops 3221225472 | bytes 2097152 | tf_op jit(solution)/shard_map/pallas_call | solution.py:127
  57.2 2.4 %collective-permute-start.16 = (f32[2,32,512]{2,1,0:T(8,128)S(1)}, f32[2,32,512]{2,1,0:T(8,128)S(1)}, u32[]{:S(2)}, u32[]{:S(2)}) collective-permute-start(f32[2,32,512]{2,1,0:T(8,128)S(1)} %get-tuple-element.43.refs_3_), channel_id=1, source_target_pairs={{1,2},{2,1},{5,6},{6,5},{9,10},{10,9},{13,14},{14,13},{17,18},{18,... | collective-permute-start | bytes 393224 | tf_op jit(solution)/shard_map/ppermute | solution.py:335
  59.7 0.2 shard_map.63.refs_4_.refs_20_.refs_8_
  59.8 0.6 collective-permute-start.24
  60.5 1.1 collective-permute-start.21
  61.6 1.9 %collective-permute-done.16.refs_5_ = f32[2,32,512]{2,1,0:T(8,128)S(1)} collective-permute-done((f32[2,32,512]{2,1,0:T(8,128)S(1)}, f32[2,32,512]{2,1,0:T(8,128)S(1)}, u32[]{:S(2)}, u32[]{:S(2)}) %collective-permute-start.16) | collective-permute-done | bytes 131104 | tf_op jit(solution)/shard_map/ppermute | solution.py:335
  63.5 0.2 shard_map.61.refs_2_.refs_20_
  63.6 0.9 collective-permute-start.22
  64.6 0.5 collective-permute-start.18
  65.1 1.2 %collective-permute-done.24.refs_8_ = f32[32,1024]{1,0:T(8,128)S(1)} collective-permute-done((f32[32,1024]{1,0:T(8,128)S(1)}, f32[32,1024]{1,0:T(8,128)S(1)}, u32[]{:S(2)}, u32[]{:S(2)}) %collective-permute-start.24) | collective-permute-done | bytes 131104 | tf_op jit(solution)/shard_map/ppermute | solution.py:285
  66.3 0.3 collective-permute-start.28
  66.6 0.7 collective-permute-start.25
  67.4 3.0 %collective-permute-done.22.refs_6_ = f32[32,1024]{1,0:T(8,128)S(1)} collective-permute-done((f32[32,1024]{1,0:T(8,128)S(1)}, f32[32,1024]{1,0:T(8,128)S(1)}, u32[]{:S(2)}, u32[]{:S(2)}) %collective-permute-start.22) | collective-permute-done | bytes 131104 | tf_op jit(solution)/shard_map/ppermute | solution.py:285
  70.3 1.4 %collective-permute-start.23 = (f32[32,1024]{1,0:T(8,128)S(1)}, f32[32,1024]{1,0:T(8,128)S(1)}, u32[]{:S(2)}, u32[]{:S(2)}) collective-permute-start(f32[32,1024]{1,0:T(8,128)S(1)} %collective-permute-done.22.refs_6_), channel_id=1, source_target_pairs={{0,4},{4,0},{8,12},{12,8},{16,20},{20,16},{24,28},{28,24},{1,5},{5... | collective-permute-start | bytes 393224 | tf_op jit(solution)/shard_map/ppermute | solution.py:282
  71.7 0.2 collective-permute-done.28.refs_12_
  71.9 0.6 collective-permute-start.32
  72.5 1.1 collective-permute-start.29
  73.7 2.9 %collective-permute-done.26.refs_10_ = f32[32,1024]{1,0:T(8,128)S(1)} collective-permute-done((f32[32,1024]{1,0:T(8,128)S(1)}, f32[32,1024]{1,0:T(8,128)S(1)}, u32[]{:S(2)}, u32[]{:S(2)}) %collective-permute-start.26) | collective-permute-done | bytes 131104 | tf_op jit(solution)/shard_map/ppermute | solution.py:285
  76.6 0.4 collective-permute-start.27
  77.0 1.8 %collective-permute-done.32.refs_16_ = f32[32,1024]{1,0:T(8,128)S(1)} collective-permute-done((f32[32,1024]{1,0:T(8,128)S(1)}, f32[32,1024]{1,0:T(8,128)S(1)}, u32[]{:S(2)}, u32[]{:S(2)}) %collective-permute-start.32) | collective-permute-done | bytes 131104 | tf_op jit(solution)/shard_map/ppermute | solution.py:285
  78.8 0.4 collective-permute-start.33
  79.1 3.1 %collective-permute-done.30.refs_14_ = f32[32,1024]{1,0:T(8,128)S(1)} collective-permute-done((f32[32,1024]{1,0:T(8,128)S(1)}, f32[32,1024]{1,0:T(8,128)S(1)}, u32[]{:S(2)}, u32[]{:S(2)}) %collective-permute-start.30) | collective-permute-done | bytes 131104 | tf_op jit(solution)/shard_map/ppermute | solution.py:285
  82.2 0.5 collective-permute-start.31
  82.7 0.8 collective-permute-done.33.refs_17_
  83.5 3.3 %collective-permute-done.31.refs_15_ = f32[32,1024]{1,0:T(8,128)S(1)} collective-permute-done((f32[32,1024]{1,0:T(8,128)S(1)}, f32[32,1024]{1,0:T(8,128)S(1)}, u32[]{:S(2)}, u32[]{:S(2)}) %collective-permute-start.31) | collective-permute-done | bytes 131104 | tf_op jit(solution)/shard_map/ppermute | solution.py:282
  86.8 6.7 %shard_map.65 = (f32[32,1024]{1,0:T(8,128)S(1)}, f32[2,32,512]{2,1,0:T(8,128)S(1)}, f32[2,32,512]{2,1,0:T(8,128)S(1)}) custom-call(s32[1]{0:T(128)} %bitcast.refs_0_, s32[16]{0:T(128)S(1)} %stack.76.refs_1_, f32[32,1024]{1,0:T(8,128)S(1)} %shard_map.61.refs_2_.refs_20_, f32[32,1024]{1,0:T(8,128)S(1)} %collective-permute-done.18.refs_3_, ...), custom_call_target="tpu_custom_call" | custom-call | flops 3221225472 | bytes 2097152 | tf_op jit(solution)/shard_map/pallas_call | solution.py:127
  93.5 7.3 %collective-permute-start.36 = (f32[2,32,512]{2,1,0:T(8,128)S(1)}, f32[2,32,512]{2,1,0:T(8,128)S(1)}, u32[]{:S(2)}, u32[]{:S(2)}) collective-permute-start(f32[2,32,512]{2,1,0:T(8,128)S(1)} %get-tuple-element.60.refs_9_), channel_id=1, source_target_pairs={{1,2},{2,1},{5,6},{6,5},{9,10},{10,9},{13,14},{14,13},{17,18},{18,... | collective-permute-start | bytes 393224 | tf_op jit(solution)/shard_map/ppermute | solution.py:335
  101.0 6.7 %shard_map.64 = (f32[32,1024]{1,0:T(8,128)S(1)}, f32[2,32,512]{2,1,0:T(8,128)S(1)}, f32[2,32,512]{2,1,0:T(8,128)S(1)}) custom-call(s32[1]{0:T(128)} %bitcast.refs_0_, s32[16]{0:T(128)S(1)} %stack.76.refs_1_, f32[32,1024]{1,0:T(8,128)S(1)} %shard_map.61.refs_2_.refs_20_, f32[32,1024]{1,0:T(8,128)S(1)} %collective-permute-done.18.refs_3_, ...), custom_call_target="tpu_custom_call" | custom-call | flops 3221225472 | bytes 2097152 | tf_op jit(solution)/shard_map/pallas_call | solution.py:127
  107.7 1.9 %collective-permute-start.34 = (f32[2,32,512]{2,1,0:T(8,128)S(1)}, f32[2,32,512]{2,1,0:T(8,128)S(1)}, u32[]{:S(2)}, u32[]{:S(2)}) collective-permute-start(f32[2,32,512]{2,1,0:T(8,128)S(1)} %get-tuple-element.57.refs_3_), channel_id=1, source_target_pairs={{1,2},{2,1},{5,6},{6,5},{9,10},{10,9},{13,14},{14,13},{17,18},{18,... | collective-permute-start | bytes 393224 | tf_op jit(solution)/shard_map/ppermute | solution.py:335
  109.7 4.3 %collective-permute-done.34.refs_5_ = f32[2,32,512]{2,1,0:T(8,128)S(1)} collective-permute-done((f32[2,32,512]{2,1,0:T(8,128)S(1)}, f32[2,32,512]{2,1,0:T(8,128)S(1)}, u32[]{:S(2)}, u32[]{:S(2)}) %collective-permute-start.34) | collective-permute-done | bytes 131104 | tf_op jit(solution)/shard_map/ppermute | solution.py:335
  114.0 1.3 %shard_map.66 = (f32[64,8,128]{2,1,0:T(8,128)}, f32[64,8,128]{2,1,0:T(8,128)}) custom-call(s32[1]{0:T(128)} %bitcast.refs_0_, f32[32,1024]{1,0:T(8,128)S(1)} %get-tuple-element.56.refs_1_, f32[32,1024]{1,0:T(8,128)S(1)} %shard_map.61.refs_2_.refs_20_, f32[2,32,512]{2,1,0:T(8,128)S(1)} %get-tuple-element.57.refs_3_, ...), custom_call_target="tpu_custom_call" | custom-call | flops 2621440 | tf_op jit(solution)/shard_map/pallas_call | solution.py:200
  (38 shorter events, 0.5 us)
Async XLA Ops:
  1.7 7.4 %collective-permute-start.2 = (f32[32,1024]{1,0:T(8,128)S(1)}, f32[32,1024]{1,0:T(8,128)S(1)}, u32[]{:S(2)}, u32[]{:S(2)}) collective-permute-start(f32[32,1024]{1,0:T(8,128)S(1)} %slice.37.refs_2_.refs_20_), channel_id=1, source_target_pairs={{0,8},{4,12},{8,16},{12,20},{16,24},{20,28},{24,0},{28,4},{1,9},{5... | collective-permute-start | bytes 393224 | tf_op jit(solution)/shard_map/ppermute | solution.py:285
  3.9 5.3 %collective-permute-start = (f32[32,1024]{1,0:T(8,128)S(1)}, f32[32,1024]{1,0:T(8,128)S(1)}, u32[]{:S(2)}, u32[]{:S(2)}) collective-permute-start(f32[32,1024]{1,0:T(8,128)S(1)} %slice.37.refs_2_.refs_20_), channel_id=1, source_target_pairs={{0,4},{4,0},{8,12},{12,8},{16,20},{20,16},{24,28},{28,24},{1,5},{5... | collective-permute-start | bytes 393224 | tf_op jit(solution)/shard_map/ppermute | solution.py:282
  5.2 5.9 %collective-permute-start.4 = (f32[32,1024]{1,0:T(8,128)S(1)}, f32[32,1024]{1,0:T(8,128)S(1)}, u32[]{:S(2)}, u32[]{:S(2)}) collective-permute-start(f32[32,1024]{1,0:T(8,128)S(1)} %slice.39.refs_4_.refs_20_.refs_2_), channel_id=1, source_target_pairs={{0,8},{4,12},{8,16},{12,20},{16,24},{20,28},{24,0},{28,4},{1,9},{5... | collective-permute-start | bytes 393224 | tf_op jit(solution)/shard_map/ppermute | solution.py:285
  6.5 4.5 %collective-permute-start.1 = (f32[32,1024]{1,0:T(8,128)S(1)}, f32[32,1024]{1,0:T(8,128)S(1)}, u32[]{:S(2)}, u32[]{:S(2)}) collective-permute-start(f32[32,1024]{1,0:T(8,128)S(1)} %slice.39.refs_4_.refs_20_.refs_2_), channel_id=1, source_target_pairs={{0,4},{4,0},{8,12},{12,8},{16,20},{20,16},{24,28},{28,24},{1,5},{5... | collective-permute-start | bytes 393224 | tf_op jit(solution)/shard_map/ppermute | solution.py:282
  9.1 11.9 %collective-permute-start.6 = (f32[32,1024]{1,0:T(8,128)S(1)}, f32[32,1024]{1,0:T(8,128)S(1)}, u32[]{:S(2)}, u32[]{:S(2)}) collective-permute-start(f32[32,1024]{1,0:T(8,128)S(1)} %collective-permute-done.2.refs_6_), channel_id=1, source_target_pairs={{0,8},{4,12},{8,16},{12,20},{16,24},{20,28},{24,0},{28,4},{1,9},{5... | collective-permute-start | bytes 393224 | tf_op jit(solution)/shard_map/ppermute | solution.py:285
  9.3 11.7 %collective-permute-start.3 = (f32[32,1024]{1,0:T(8,128)S(1)}, f32[32,1024]{1,0:T(8,128)S(1)}, u32[]{:S(2)}, u32[]{:S(2)}) collective-permute-start(f32[32,1024]{1,0:T(8,128)S(1)} %collective-permute-done.2.refs_6_), channel_id=1, source_target_pairs={{0,4},{4,0},{8,12},{12,8},{16,20},{20,16},{24,28},{28,24},{1,5},{5... | collective-permute-start | bytes 393224 | tf_op jit(solution)/shard_map/ppermute | solution.py:282
  11.1 12.0 %collective-permute-start.8 = (f32[32,1024]{1,0:T(8,128)S(1)}, f32[32,1024]{1,0:T(8,128)S(1)}, u32[]{:S(2)}, u32[]{:S(2)}) collective-permute-start(f32[32,1024]{1,0:T(8,128)S(1)} %collective-permute-done.4.refs_8_), channel_id=1, source_target_pairs={{0,8},{4,12},{8,16},{12,20},{16,24},{20,28},{24,0},{28,4},{1,9},{5... | collective-permute-start | bytes 393224 | tf_op jit(solution)/shard_map/ppermute | solution.py:285
  12.1 11.0 %collective-permute-start.5 = (f32[32,1024]{1,0:T(8,128)S(1)}, f32[32,1024]{1,0:T(8,128)S(1)}, u32[]{:S(2)}, u32[]{:S(2)}) collective-permute-start(f32[32,1024]{1,0:T(8,128)S(1)} %collective-permute-done.4.refs_8_), channel_id=1, source_target_pairs={{0,4},{4,0},{8,12},{12,8},{16,20},{20,16},{24,28},{28,24},{1,5},{5... | collective-permute-start | bytes 393224 | tf_op jit(solution)/shard_map/ppermute | solution.py:282
  15.2 9.3 %collective-permute-start.14 = (f32[33,4,128]{2,1,0:T(4,128)S(1)}, f32[33,4,128]{2,1,0:T(4,128)S(1)}, u32[]{:S(2)}, u32[]{:S(2)}) collective-permute-start(f32[33,4,128]{2,1,0:T(4,128)S(1)} %pad_maximum_fusion), channel_id=1, source_target_pairs={{0,1},{1,2},{2,3},{4,5},{5,6},{6,7},{8,9},{9,10},{10,11},{12,13},{... | collective-permute-start | bytes 202760 | tf_op jit(solution)/shard_map/ppermute | solution.py:317
  21.0 11.0 %collective-permute-start.10 = (f32[32,1024]{1,0:T(8,128)S(1)}, f32[32,1024]{1,0:T(8,128)S(1)}, u32[]{:S(2)}, u32[]{:S(2)}) collective-permute-start(f32[32,1024]{1,0:T(8,128)S(1)} %collective-permute-done.6.refs_10_), channel_id=1, source_target_pairs={{0,8},{4,12},{8,16},{12,20},{16,24},{20,28},{24,0},{28,4},{1,9},{5... | collective-permute-start | bytes 393224 | tf_op jit(solution)/shard_map/ppermute | solution.py:285
  22.9 9.1 %collective-permute-start.7 = (f32[32,1024]{1,0:T(8,128)S(1)}, f32[32,1024]{1,0:T(8,128)S(1)}, u32[]{:S(2)}, u32[]{:S(2)}) collective-permute-start(f32[32,1024]{1,0:T(8,128)S(1)} %collective-permute-done.6.refs_10_), channel_id=1, source_target_pairs={{0,4},{4,0},{8,12},{12,8},{16,20},{20,16},{24,28},{28,24},{1,5},{5... | collective-permute-start | bytes 393224 | tf_op jit(solution)/shard_map/ppermute | solution.py:282
  23.1 9.8 %collective-permute-start.12 = (f32[32,1024]{1,0:T(8,128)S(1)}, f32[32,1024]{1,0:T(8,128)S(1)}, u32[]{:S(2)}, u32[]{:S(2)}) collective-permute-start(f32[32,1024]{1,0:T(8,128)S(1)} %collective-permute-done.8.refs_12_), channel_id=1, source_target_pairs={{0,8},{4,12},{8,16},{12,20},{16,24},{20,28},{24,0},{28,4},{1,9},{5... | collective-permute-start | bytes 393224 | tf_op jit(solution)/shard_map/ppermute | solution.py:285
  23.8 9.1 %collective-permute-start.9 = (f32[32,1024]{1,0:T(8,128)S(1)}, f32[32,1024]{1,0:T(8,128)S(1)}, u32[]{:S(2)}, u32[]{:S(2)}) collective-permute-start(f32[32,1024]{1,0:T(8,128)S(1)} %collective-permute-done.8.refs_12_), channel_id=1, source_target_pairs={{0,4},{4,0},{8,12},{12,8},{16,20},{20,16},{24,28},{28,24},{1,5},{5... | collective-permute-start | bytes 393224 | tf_op jit(solution)/shard_map/ppermute | solution.py:282
  24.4 5.6 %collective-permute-start.15 = (f32[33,4,128]{2,1,0:T(4,128)S(1)}, f32[33,4,128]{2,1,0:T(4,128)S(1)}, u32[]{:S(2)}, u32[]{:S(2)}) collective-permute-start(f32[33,4,128]{2,1,0:T(4,128)S(1)} %pad_maximum_fusion.1), channel_id=1, source_target_pairs={{1,0},{2,1},{3,2},{5,4},{6,5},{7,6},{9,8},{10,9},{11,10},{13,12},{... | collective-permute-start | bytes 202760 | tf_op jit(solution)/shard_map/ppermute | solution.py:318
  30.0 0.9 copy-start
  32.0 4.7 %collective-permute-start.11 = (f32[32,1024]{1,0:T(8,128)S(1)}, f32[32,1024]{1,0:T(8,128)S(1)}, u32[]{:S(2)}, u32[]{:S(2)}) collective-permute-start(f32[32,1024]{1,0:T(8,128)S(1)} %collective-permute-done.10.refs_14_), channel_id=1, source_target_pairs={{0,4},{4,0},{8,12},{12,8},{16,20},{20,16},{24,28},{28,24},{1,5},{5... | collective-permute-start | bytes 393224 | tf_op jit(solution)/shard_map/ppermute | solution.py:282
  32.9 5.2 %collective-permute-start.13 = (f32[32,1024]{1,0:T(8,128)S(1)}, f32[32,1024]{1,0:T(8,128)S(1)}, u32[]{:S(2)}, u32[]{:S(2)}) collective-permute-start(f32[32,1024]{1,0:T(8,128)S(1)} %collective-permute-done.12.refs_16_), channel_id=1, source_target_pairs={{0,4},{4,0},{8,12},{12,8},{16,20},{20,16},{24,28},{28,24},{1,5},{5... | collective-permute-start | bytes 393224 | tf_op jit(solution)/shard_map/ppermute | solution.py:282
  38.1 2.2 %copy-start.1 = (f32[32,64,512]{2,1,0:T(8,128)S(1)}, f32[32,64,512]{2,1,0:T(8,128)}, u32[]{:S(2)}) copy-start(f32[32,64,512]{2,1,0:T(8,128)} %param.7) | copy-start | bytes 12582916
  47.0 12.7 %collective-permute-start.19 = (f32[2,32,512]{2,1,0:T(8,128)S(1)}, f32[2,32,512]{2,1,0:T(8,128)S(1)}, u32[]{:S(2)}, u32[]{:S(2)}) collective-permute-start(f32[2,32,512]{2,1,0:T(8,128)S(1)} %get-tuple-element.48.refs_3_), channel_id=1, source_target_pairs={{1,2},{2,1},{5,6},{6,5},{9,10},{10,9},{13,14},{14,13},{17,18},{18,... | collective-permute-start | bytes 393224 | tf_op jit(solution)/shard_map/ppermute | solution.py:335
  50.4 36.5 %copy-start.2 = (f32[32,64,512]{2,1,0:T(8,128)S(1)}, f32[32,64,512]{2,1,0:T(8,128)}, u32[]{:S(2)}) copy-start(f32[32,64,512]{2,1,0:T(8,128)} %param.7) | copy-start | bytes 12582916
  50.4 9.3 %collective-permute-start.20 = (f32[2,32,512]{2,1,0:T(8,128)S(1)}, f32[2,32,512]{2,1,0:T(8,128)S(1)}, u32[]{:S(2)}, u32[]{:S(2)}) collective-permute-start(f32[2,32,512]{2,1,0:T(8,128)S(1)} %get-tuple-element.49.refs_4_), channel_id=1, source_target_pairs={{0,1},{2,3},{1,0},{3,2},{4,5},{6,7},{5,4},{7,6},{8,9},{10,11},{9,8... | collective-permute-start | bytes 393224 | tf_op jit(solution)/shard_map/ppermute | solution.py:334
  57.2 6.3 %collective-permute-start.16 = (f32[2,32,512]{2,1,0:T(8,128)S(1)}, f32[2,32,512]{2,1,0:T(8,128)S(1)}, u32[]{:S(2)}, u32[]{:S(2)}) collective-permute-start(f32[2,32,512]{2,1,0:T(8,128)S(1)} %get-tuple-element.43.refs_3_), channel_id=1, source_target_pairs={{1,2},{2,1},{5,6},{6,5},{9,10},{10,9},{13,14},{14,13},{17,18},{18,... | collective-permute-start | bytes 393224 | tf_op jit(solution)/shard_map/ppermute | solution.py:335
  59.6 3.9 %collective-permute-start.17 = (f32[2,32,512]{2,1,0:T(8,128)S(1)}, f32[2,32,512]{2,1,0:T(8,128)S(1)}, u32[]{:S(2)}, u32[]{:S(2)}) collective-permute-start(f32[2,32,512]{2,1,0:T(8,128)S(1)} %get-tuple-element.44.refs_4_), channel_id=1, source_target_pairs={{0,1},{2,3},{1,0},{3,2},{4,5},{6,7},{5,4},{7,6},{8,9},{10,11},{9,8... | collective-permute-start | bytes 393224 | tf_op jit(solution)/shard_map/ppermute | solution.py:334
  59.8 6.4 %collective-permute-start.24 = (f32[32,1024]{1,0:T(8,128)S(1)}, f32[32,1024]{1,0:T(8,128)S(1)}, u32[]{:S(2)}, u32[]{:S(2)}) collective-permute-start(f32[32,1024]{1,0:T(8,128)S(1)} %shard_map.63.refs_4_.refs_20_.refs_8_), channel_id=1, source_target_pairs={{0,8},{4,12},{8,16},{12,20},{16,24},{20,28},{24,0},{28,4},{1,9},{5... | collective-permute-start | bytes 393224 | tf_op jit(solution)/shard_map/ppermute | solution.py:285
  60.5 5.8 %collective-permute-start.21 = (f32[32,1024]{1,0:T(8,128)S(1)}, f32[32,1024]{1,0:T(8,128)S(1)}, u32[]{:S(2)}, u32[]{:S(2)}) collective-permute-start(f32[32,1024]{1,0:T(8,128)S(1)} %shard_map.63.refs_4_.refs_20_.refs_8_), channel_id=1, source_target_pairs={{0,4},{4,0},{8,12},{12,8},{16,20},{20,16},{24,28},{28,24},{1,5},{5... | collective-permute-start | bytes 393224 | tf_op jit(solution)/shard_map/ppermute | solution.py:282
  63.6 6.7 %collective-permute-start.22 = (f32[32,1024]{1,0:T(8,128)S(1)}, f32[32,1024]{1,0:T(8,128)S(1)}, u32[]{:S(2)}, u32[]{:S(2)}) collective-permute-start(f32[32,1024]{1,0:T(8,128)S(1)} %shard_map.61.refs_2_.refs_20_), channel_id=1, source_target_pairs={{0,8},{4,12},{8,16},{12,20},{16,24},{20,28},{24,0},{28,4},{1,9},{5... | collective-permute-start | bytes 393224 | tf_op jit(solution)/shard_map/ppermute | solution.py:285
  64.6 5.7 %collective-permute-start.18 = (f32[32,1024]{1,0:T(8,128)S(1)}, f32[32,1024]{1,0:T(8,128)S(1)}, u32[]{:S(2)}, u32[]{:S(2)}) collective-permute-start(f32[32,1024]{1,0:T(8,128)S(1)} %shard_map.61.refs_2_.refs_20_), channel_id=1, source_target_pairs={{0,4},{4,0},{8,12},{12,8},{16,20},{20,16},{24,28},{28,24},{1,5},{5... | collective-permute-start | bytes 393224 | tf_op jit(solution)/shard_map/ppermute | solution.py:282
  66.3 5.6 %collective-permute-start.28 = (f32[32,1024]{1,0:T(8,128)S(1)}, f32[32,1024]{1,0:T(8,128)S(1)}, u32[]{:S(2)}, u32[]{:S(2)}) collective-permute-start(f32[32,1024]{1,0:T(8,128)S(1)} %collective-permute-done.24.refs_8_), channel_id=1, source_target_pairs={{0,8},{4,12},{8,16},{12,20},{16,24},{20,28},{24,0},{28,4},{1,9},{5... | collective-permute-start | bytes 393224 | tf_op jit(solution)/shard_map/ppermute | solution.py:285
  66.6 5.3 %collective-permute-start.25 = (f32[32,1024]{1,0:T(8,128)S(1)}, f32[32,1024]{1,0:T(8,128)S(1)}, u32[]{:S(2)}, u32[]{:S(2)}) collective-permute-start(f32[32,1024]{1,0:T(8,128)S(1)} %collective-permute-done.24.refs_8_), channel_id=1, source_target_pairs={{0,4},{4,0},{8,12},{12,8},{16,20},{20,16},{24,28},{28,24},{1,5},{5... | collective-permute-start | bytes 393224 | tf_op jit(solution)/shard_map/ppermute | solution.py:282
  70.3 6.3 %collective-permute-start.26 = (f32[32,1024]{1,0:T(8,128)S(1)}, f32[32,1024]{1,0:T(8,128)S(1)}, u32[]{:S(2)}, u32[]{:S(2)}) collective-permute-start(f32[32,1024]{1,0:T(8,128)S(1)} %collective-permute-done.22.refs_6_), channel_id=1, source_target_pairs={{0,8},{4,12},{8,16},{12,20},{16,24},{20,28},{24,0},{28,4},{1,9},{5... | collective-permute-start | bytes 393224 | tf_op jit(solution)/shard_map/ppermute | solution.py:285
  70.3 6.3 %collective-permute-start.23 = (f32[32,1024]{1,0:T(8,128)S(1)}, f32[32,1024]{1,0:T(8,128)S(1)}, u32[]{:S(2)}, u32[]{:S(2)}) collective-permute-start(f32[32,1024]{1,0:T(8,128)S(1)} %collective-permute-done.22.refs_6_), channel_id=1, source_target_pairs={{0,4},{4,0},{8,12},{12,8},{16,20},{20,16},{24,28},{28,24},{1,5},{5... | collective-permute-start | bytes 393224 | tf_op jit(solution)/shard_map/ppermute | solution.py:282
  71.9 6.9 %collective-permute-start.32 = (f32[32,1024]{1,0:T(8,128)S(1)}, f32[32,1024]{1,0:T(8,128)S(1)}, u32[]{:S(2)}, u32[]{:S(2)}) collective-permute-start(f32[32,1024]{1,0:T(8,128)S(1)} %collective-permute-done.28.refs_12_), channel_id=1, source_target_pairs={{0,8},{4,12},{8,16},{12,20},{16,24},{20,28},{24,0},{28,4},{1,9},{5... | collective-permute-start | bytes 393224 | tf_op jit(solution)/shard_map/ppermute | solution.py:285
  72.5 6.3 %collective-permute-start.29 = (f32[32,1024]{1,0:T(8,128)S(1)}, f32[32,1024]{1,0:T(8,128)S(1)}, u32[]{:S(2)}, u32[]{:S(2)}) collective-permute-start(f32[32,1024]{1,0:T(8,128)S(1)} %collective-permute-done.28.refs_12_), channel_id=1, source_target_pairs={{0,4},{4,0},{8,12},{12,8},{16,20},{20,16},{24,28},{28,24},{1,5},{5... | collective-permute-start | bytes 393224 | tf_op jit(solution)/shard_map/ppermute | solution.py:282
  76.6 5.6 %collective-permute-start.30 = (f32[32,1024]{1,0:T(8,128)S(1)}, f32[32,1024]{1,0:T(8,128)S(1)}, u32[]{:S(2)}, u32[]{:S(2)}) collective-permute-start(f32[32,1024]{1,0:T(8,128)S(1)} %collective-permute-done.26.refs_10_), channel_id=1, source_target_pairs={{0,8},{4,12},{8,16},{12,20},{16,24},{20,28},{24,0},{28,4},{1,9},{5... | collective-permute-start | bytes 393224 | tf_op jit(solution)/shard_map/ppermute | solution.py:285
  76.6 5.6 %collective-permute-start.27 = (f32[32,1024]{1,0:T(8,128)S(1)}, f32[32,1024]{1,0:T(8,128)S(1)}, u32[]{:S(2)}, u32[]{:S(2)}) collective-permute-start(f32[32,1024]{1,0:T(8,128)S(1)} %collective-permute-done.26.refs_10_), channel_id=1, source_target_pairs={{0,4},{4,0},{8,12},{12,8},{16,20},{20,16},{24,28},{28,24},{1,5},{5... | collective-permute-start | bytes 393224 | tf_op jit(solution)/shard_map/ppermute | solution.py:282
  78.8 4.8 %collective-permute-start.33 = (f32[32,1024]{1,0:T(8,128)S(1)}, f32[32,1024]{1,0:T(8,128)S(1)}, u32[]{:S(2)}, u32[]{:S(2)}) collective-permute-start(f32[32,1024]{1,0:T(8,128)S(1)} %collective-permute-done.32.refs_16_), channel_id=1, source_target_pairs={{0,4},{4,0},{8,12},{12,8},{16,20},{20,16},{24,28},{28,24},{1,5},{5... | collective-permute-start | bytes 393224 | tf_op jit(solution)/shard_map/ppermute | solution.py:282
  82.2 4.6 %collective-permute-start.31 = (f32[32,1024]{1,0:T(8,128)S(1)}, f32[32,1024]{1,0:T(8,128)S(1)}, u32[]{:S(2)}, u32[]{:S(2)}) collective-permute-start(f32[32,1024]{1,0:T(8,128)S(1)} %collective-permute-done.30.refs_14_), channel_id=1, source_target_pairs={{0,4},{4,0},{8,12},{12,8},{16,20},{20,16},{24,28},{28,24},{1,5},{5... | collective-permute-start | bytes 393224 | tf_op jit(solution)/shard_map/ppermute | solution.py:282
  93.5 16.2 %collective-permute-start.36 = (f32[2,32,512]{2,1,0:T(8,128)S(1)}, f32[2,32,512]{2,1,0:T(8,128)S(1)}, u32[]{:S(2)}, u32[]{:S(2)}) collective-permute-start(f32[2,32,512]{2,1,0:T(8,128)S(1)} %get-tuple-element.60.refs_9_), channel_id=1, source_target_pairs={{1,2},{2,1},{5,6},{6,5},{9,10},{10,9},{13,14},{14,13},{17,18},{18,... | collective-permute-start | bytes 393224 | tf_op jit(solution)/shard_map/ppermute | solution.py:335
  100.9 8.8 %collective-permute-start.37 = (f32[2,32,512]{2,1,0:T(8,128)S(1)}, f32[2,32,512]{2,1,0:T(8,128)S(1)}, u32[]{:S(2)}, u32[]{:S(2)}) collective-permute-start(f32[2,32,512]{2,1,0:T(8,128)S(1)} %get-tuple-element.61.refs_10_), channel_id=1, source_target_pairs={{0,1},{2,3},{1,0},{3,2},{4,5},{6,7},{5,4},{7,6},{8,9},{10,11},{9,8... | collective-permute-start | bytes 393224 | tf_op jit(solution)/shard_map/ppermute | solution.py:334
  107.7 6.3 %collective-permute-start.34 = (f32[2,32,512]{2,1,0:T(8,128)S(1)}, f32[2,32,512]{2,1,0:T(8,128)S(1)}, u32[]{:S(2)}, u32[]{:S(2)}) collective-permute-start(f32[2,32,512]{2,1,0:T(8,128)S(1)} %get-tuple-element.57.refs_3_), channel_id=1, source_target_pairs={{1,2},{2,1},{5,6},{6,5},{9,10},{10,9},{13,14},{14,13},{17,18},{18,... | collective-permute-start | bytes 393224 | tf_op jit(solution)/shard_map/ppermute | solution.py:335
  109.6 4.4 %collective-permute-start.35 = (f32[2,32,512]{2,1,0:T(8,128)S(1)}, f32[2,32,512]{2,1,0:T(8,128)S(1)}, u32[]{:S(2)}, u32[]{:S(2)}) collective-permute-start(f32[2,32,512]{2,1,0:T(8,128)S(1)} %get-tuple-element.58.refs_4_), channel_id=1, source_target_pairs={{0,1},{2,3},{1,0},{3,2},{4,5},{6,7},{5,4},{7,6},{8,9},{10,11},{9,8... | collective-permute-start | bytes 393224 | tf_op jit(solution)/shard_map/ppermute | solution.py:334
where the time goes:
time: 116 us; the launch traced here: 115 us
  starting transfers between devices  45.5 us (39%)
  waiting for transfers between devices  32.4 us (28%)
  Pallas kernels  29.4 us (25%)
  local copies, waits for them, and re-layouts  6.96 us (6%)
    pallas_call x4, Pallas kernels, mix(): pl.pallas_call(lambda *refs: mix_kernel(planes, half, len(blocks), *refs)...  26.8 us
    ppermute x4, starting transfers between devices, on_device(): odd_in = lax.ppermute(odd_own, 'space', swap_odd)  15 us
    ppermute x12, waiting for transfers between devices, gathered(): current[h] = after(lax.ppermute(sent[h], 'mode', ring), block)  15 us
    ppermute x16, starting transfers between devices, gathered(): block = lax.ppermute(block, 'mode', turned)  12.6 us
    ppermute x12, starting transfers between devices, gathered(): current[h] = after(lax.ppermute(sent[h], 'mode', ring), block)  9.79 us
    ppermute x16, waiting for transfers between devices, gathered(): block = lax.ppermute(block, 'mode', turned)  7.61 us
    ppermute x4, waiting for transfers between devices, on_device(): odd_in = lax.ppermute(odd_own, 'space', swap_odd)  6.15 us
    ppermute x1, starting transfers between devices, on_device(): lax.ppermute(jnp.concatenate([coefficients[:, planes - 1], coefficients[:...  5.82 us
  transfers between devices with their start and end apart: 38, of which 15 were waited for; matrix products, arithmetic and copies ran while one was open for 3% of the time, Pallas kernels for 13%

commit v1 on v0

--- a/solution.py
+++ b/solution.py
@@ -39,17 +39,18 @@
     return jnp.where(lane == edge, 0.0, moved)
 
 
-def mix_kernel(planes, half, count, odd, offsets, *refs):
+def mix_kernel(planes, count, odd, offsets, *refs):
     blocks, refs = refs[:count], refs[count:]
     c_ref, w_ref, press, source, part_ref, odd_ref, even_ref, field_ref, u_ref, cs_ref, sems = refs
     rows, lanes_all = press.shape
     cells = lanes_all // planes
     terms = w_ref.shape[1]
     chunk = terms // sems.shape[0]
+    group = 32 if rows % 32 == 0 else rows
 
     copies = [
         pltpu.make_async_copy(
-            c_ref.at[pl.ds(k, chunk), half], cs_ref.at[pl.ds(k, chunk)], sems.at[k // chunk]
+            c_ref.at[pl.ds(k, chunk)], cs_ref.at[pl.ds(k, chunk)], sems.at[k // chunk]
         )
         for k in range(0, terms, chunk)
     ]
@@ -69,14 +70,16 @@
     def weigh(start, t, m):
         for r in range(tile // LANES):
             lanes = slice(t * tile + r * LANES, t * tile + (r + 1) * LANES)
-            total = [None if start == 0 else field_ref[n, :, lanes] for n in range(KINDS)]
-            for k in range(chunk):
-                value = m[k * rows : (k + 1) * rows, r * LANES : (r + 1) * LANES]
+            for g in range(0, rows, group):
+                some = slice(g, g + group)
+                total = [None if start == 0 else field_ref[n, some, lanes] for n in range(KINDS)]
+                for k in range(chunk):
+                    value = m[k * rows + g : k * rows + g + group, r * LANES : (r + 1) * LANES]
+                    for n in range(KINDS):
+                        term = w_ref[n, start + k : start + k + 1, lanes] * value
+                        total[n] = term if total[n] is None else total[n] + term
                 for n in range(KINDS):
-                    term = w_ref[n, start + k : start + k + 1, lanes] * value
-                    total[n] = term if total[n] is None else total[n] + term
-            for n in range(KINDS):
-                field_ref[n, :, lanes] = total[n]
+                    field_ref[n, some, lanes] = total[n]
 
     before = None
     for k in range(0, terms, chunk):
@@ -118,14 +121,14 @@
         even_ref[at] = jnp.where(is_odd, low, high)
 
 
-def mix(odd, offsets, blocks, c, w, press, source, half, planes):
+def mix(odd, offsets, blocks, c, w, press, source, planes):
     rows, lanes_all = press.shape
     cells = lanes_all // planes
-    terms, _, _, modes = c.shape
+    terms, _, modes = c.shape
     chunks = max(1, terms * rows // 256)
     sent = jax.ShapeDtypeStruct((2, rows, cells), jnp.float32)
     return pl.pallas_call(
-        lambda *refs: mix_kernel(planes, half, len(blocks), *refs),
+        lambda *refs: mix_kernel(planes, len(blocks), *refs),
         in_specs=[SMEM] * 2 + [VMEM] * len(blocks) + [pl.BlockSpec(memory_space=pltpu.HBM)] + [VMEM] * 3,
         out_specs=[VMEM] * 3,
         out_shape=[jax.ShapeDtypeStruct(press.shape, jnp.float32), sent, sent],
@@ -135,7 +138,7 @@
             pltpu.VMEM((terms, rows, modes), jnp.float32),
             pltpu.SemaphoreType.DMA((chunks,)),
         ],
-        compiler_params=pltpu.CompilerParams(vmem_limit_bytes=20 * 2**20),
+        compiler_params=pltpu.CompilerParams(vmem_limit_bytes=24 * 2**20),
         cost_estimate=pl.CostEstimate(
             flops=6 * terms * rows * modes * lanes_all, bytes_accessed=4 * terms * rows * modes, transcendentals=0
         ),
@@ -268,19 +271,20 @@
     return lax.optimization_barrier((x, *others))[0] if others else x
 
 
-def gathered(halves, inner, outer):
+def gathered(whole, halves, inner, outer):
     size = inner * outer
+    rows = whole.shape[0] // halves
     ring = [(i, (i + inner) % size) for i in range(size)]
     turned = [(i, i // inner * inner + (i % inner + 1) % inner) for i in range(size)]
     found = []
-    current = list(halves)
+    current = [whole[h * rows : (h + 1) * rows] for h in range(halves)]
     for step in range(outer):
         sent = list(current)
         for h, block in enumerate(sent):
-            found.append((block, step, 0, h))
+            found.append((block, step, 0, h * rows))
             for turn in range(1, inner):
                 block = lax.ppermute(block, "mode", turned)
-                found.append((block, step, turn, h))
+                found.append((block, step, turn, h * rows))
             if step < outer - 1:
                 current[h] = after(lax.ppermute(sent[h], "mode", ring), block)
     return found
@@ -294,20 +298,19 @@
     inner = max(1, LANES // own)
     outer = size // inner
     halves = 2 if own % 32 == 0 else 1
-    rows = own // halves
 
     flat = pressure.reshape(own, planes * cells)
-    press = [flat[h * rows : (h + 1) * rows] for h in range(halves)]
-    found = gathered(press, inner, outer)
+    press = flat
+    found = gathered(press, halves, inner, outer)
     mode_at = lax.axis_index("mode")
     outer_at, inner_at = mode_at // inner, mode_at % inner
     offsets = jnp.stack(
         [
-            ((outer_at - f[1] + outer) % outer * inner + (inner_at - f[2] + inner) % inner) * own + f[3] * rows
+            ((outer_at - f[1] + outer) % outer * inner + (inner_at - f[2] + inner) % inner) * own + f[3]
             for f in found
         ]
     ).astype(jnp.int32)
-    c = coupling.reshape(terms, halves, rows, size * own)
+    c = coupling
 
     coefficients = after(coefficients, found[inner - 1][0])
     source = after(source, found[2 * inner * halves][0])
@@ -318,27 +321,24 @@
     high = lax.ppermute(jnp.concatenate([coefficients[:, 0], coefficients[:1, 1]]), "space", down)
     slab = lax.axis_index("space")
     beside = jnp.stack([slab > 0, slab < slabs - 1]).astype(jnp.int32)
+    beside = after(beside, found[-inner * halves][0])
     w, w0, inv = all_weights(beside, coefficients, low, high)
 
     odd = (slab % 2).astype(jnp.int32).reshape(1)
     pairs = [[(i, i + 1) for i in range(start, slabs - 1, 2)] for start in (1, 0)]
     swap_odd, swap_even = [p + [(j, i) for i, j in p] for p in pairs]
 
-    flat = source.reshape(own, planes * cells)
-    src = [flat[h * rows : (h + 1) * rows] for h in range(halves)]
+    src = source.reshape(own, planes * cells)
     for step in range(ITERS):
-        blocks = [f[0] for f in found]
-        states = []
-        for h in range(halves):
-            part, odd_own, even_own = mix(odd, offsets, blocks, c, w, press[h], src[h], h, planes)
-            even_in = lax.ppermute(even_own, "space", swap_even)
-            odd_in = lax.ppermute(odd_own, "space", swap_odd)
-            states.append((part, press[h], odd_own, even_own, odd_in, even_in))
+        part, odd_own, even_own = mix(odd, offsets, [f[0] for f in found], c, w, press, src, planes)
+        odd_in = lax.ppermute(odd_own, "space", swap_odd)
+        even_in = lax.ppermute(even_own, "space", swap_even)
+        state = (part, press, odd_own, even_own, odd_in, even_in)
         if step < ITERS - 1:
-            press = [smooth(odd, [state], w0, inv, False)[0] for state in states]
-            found = gathered(press, inner, outer)
+            press = smooth(odd, [state], w0, inv, False)[0]
+            found = gathered(press, halves, inner, outer)
         else:
-            outs = smooth(odd, states, w0, inv, True)
+            outs = smooth(odd, [state], w0, inv, True)
     return tuple(x.reshape(pressure.shape) for x in outs)
 
 

time: 116 us -> 110 us (0.948)
  waiting for transfers between devices: 32.4 us -> 29.5 us
  Pallas kernels: 29.4 us -> 27.1 us
  starting transfers between devices: 45.5 us -> 43.5 us
    ppermute x4 -> x2, starting transfers between devices: 15 us -> 7.61 us  [on_device(): odd_in = lax.ppermute(odd_own, 'space', swap_odd)]
    ppermute x4 -> x2, waiting for transfers between devices: 6.15 us -> 9.94 us  [on_device(): odd_in = lax.ppermute(odd_own, 'space', swap_odd)]
    ppermute x16, starting transfers between devices: 12.6 us -> 16.3 us  [gathered(): block = lax.ppermute(block, 'mode', turned)]
    ppermute x16, waiting for transfers between devices: 7.61 us -> 4.1 us  [gathered(): block = lax.ppermute(block, 'mode', turned)]
    pallas_call x4 -> x2, Pallas kernels: 26.8 us -> 24.5 us  [mix(): pl.pallas_call(lambda *refs: mix_kernel(planes, len(blocks), *refs), in_s...]
    reshape x0 -> x2, local copies, waits for them, and re-layouts: none -> 2.11 us  [the longest x1 1.05 us: on_device(): src = source.reshape(own, planes * cells)]
    ppermute x1, waiting for transfers between devices: 3.6 us -> 1.91 us  [on_device(): lax.ppermute(jnp.concatenate([coefficients[:, 0], coefficients[:1, 1]]),...]
    ppermute x1, starting transfers between devices: 5.82 us -> 7.43 us  [on_device(): lax.ppermute(jnp.concatenate([coefficients[:, planes - 1], coefficients[:...]
  transfers between devices with their start and end apart: 38 -> 34, of which waited for: 15 -> 14; matrix products, arithmetic and copies ran while one was open for 3% -> 4% of each run, Pallas kernels for 13% -> 1%
where the time goes in v1:
time: 110 us; the launch traced here: 109 us
  starting transfers between devices  43.5 us (40%)
  waiting for transfers between devices  29.5 us (27%)
  Pallas kernels  27.1 us (25%)
  local copies, waits for them, and re-layouts  7.99 us (7%)
    pallas_call x2, Pallas kernels, mix(): pl.pallas_call(lambda *refs: mix_kernel(planes, len(blocks), *refs), in_s...  24.5 us
    ppermute x16, starting transfers between devices, gathered(): block = lax.ppermute(block, 'mode', turned)  16.3 us
    ppermute x12, waiting for transfers between devices, gathered(): current[h] = after(lax.ppermute(sent[h], 'mode', ring), block)  13.6 us
    ppermute x2, waiting for transfers between devices, on_device(): odd_in = lax.ppermute(odd_own, 'space', swap_odd)  9.94 us
    ppermute x12, starting transfers between devices, gathered(): current[h] = after(lax.ppermute(sent[h], 'mode', ring), block)  9.47 us
    ppermute x2, starting transfers between devices, on_device(): odd_in = lax.ppermute(odd_own, 'space', swap_odd)  7.61 us
    ppermute x1, starting transfers between devices, on_device(): lax.ppermute(jnp.concatenate([coefficients[:, planes - 1], coefficients[:...  7.43 us
    ppermute x16, waiting for transfers between devices, gathered(): block = lax.ppermute(block, 'mode', turned)  4.1 us
  transfers between devices with their start and end apart: 34, of which 14 were waited for; matrix products, arithmetic and copies ran while one was open for 4% of the time, Pallas kernels for 1%

profile of v1, /device:TPU:1, one launch (start us, length us, event | category | flops | bytes accessed | tf_op | source)
XLA Modules:
  0.0 109.1 jit_solution(9247655692432597769)
XLA Ops:
  0.6 1.0 fusion.1
  1.6 0.1 slice.31.refs_2_
  1.7 2.2 %collective-permute-start.2 = (f32[32,1024]{1,0:T(8,128)S(1)}, f32[32,1024]{1,0:T(8,128)S(1)}, u32[]{:S(2)}, u32[]{:S(2)}) collective-permute-start(f32[32,1024]{1,0:T(8,128)S(1)} %slice.31.refs_2_), channel_id=1, source_target_pairs={{0,8},{4,12},{8,16},{12,20},{16,24},{20,28},{24,0},{28,4},{1,9},{5... | collective-permute-start | bytes 393224 | tf_op jit(solution)/shard_map/ppermute | solution.py:289
  3.9 1.2 %collective-permute-start = (f32[32,1024]{1,0:T(8,128)S(1)}, f32[32,1024]{1,0:T(8,128)S(1)}, u32[]{:S(2)}, u32[]{:S(2)}) collective-permute-start(f32[32,1024]{1,0:T(8,128)S(1)} %slice.31.refs_2_), channel_id=1, source_target_pairs={{0,4},{4,0},{8,12},{12,8},{16,20},{20,16},{24,28},{28,24},{1,5},{5... | collective-permute-start | bytes 393224 | tf_op jit(solution)/shard_map/ppermute | solution.py:286
  5.1 0.1 slice.33.refs_4_
  5.2 1.3 %collective-permute-start.4 = (f32[32,1024]{1,0:T(8,128)S(1)}, f32[32,1024]{1,0:T(8,128)S(1)}, u32[]{:S(2)}, u32[]{:S(2)}) collective-permute-start(f32[32,1024]{1,0:T(8,128)S(1)} %slice.33.refs_4_), channel_id=1, source_target_pairs={{0,8},{4,12},{8,16},{12,20},{16,24},{20,28},{24,0},{28,4},{1,9},{5... | collective-permute-start | bytes 393224 | tf_op jit(solution)/shard_map/ppermute | solution.py:289
  6.5 0.2 collective-permute-start.1
  6.7 1.1 reshape.26.refs_20_.refs_2_
  7.8 0.1 stack.76.refs_1_
  7.9 1.2 %collective-permute-done.2.refs_6_ = f32[32,1024]{1,0:T(8,128)S(1)} collective-permute-done((f32[32,1024]{1,0:T(8,128)S(1)}, f32[32,1024]{1,0:T(8,128)S(1)}, u32[]{:S(2)}, u32[]{:S(2)}) %collective-permute-start.2) | collective-permute-done | bytes 131104 | tf_op jit(solution)/shard_map/ppermute | solution.py:289
  9.1 0.2 collective-permute-start.6
  9.3 1.2 %collective-permute-start.3 = (f32[32,1024]{1,0:T(8,128)S(1)}, f32[32,1024]{1,0:T(8,128)S(1)}, u32[]{:S(2)}, u32[]{:S(2)}) collective-permute-start(f32[32,1024]{1,0:T(8,128)S(1)} %collective-permute-done.2.refs_6_), channel_id=1, source_target_pairs={{0,4},{4,0},{8,12},{12,8},{16,20},{20,16},{24,28},{28,24},{1,5},{5... | collective-permute-start | bytes 393224 | tf_op jit(solution)/shard_map/ppermute | solution.py:286
  10.5 0.5 collective-permute-done.4.refs_8_
  11.1 1.0 collective-permute-start.8
  12.1 1.5 %collective-permute-start.5 = (f32[32,1024]{1,0:T(8,128)S(1)}, f32[32,1024]{1,0:T(8,128)S(1)}, u32[]{:S(2)}, u32[]{:S(2)}) collective-permute-start(f32[32,1024]{1,0:T(8,128)S(1)} %collective-permute-done.4.refs_8_), channel_id=1, source_target_pairs={{0,4},{4,0},{8,12},{12,8},{16,20},{20,16},{24,28},{28,24},{1,5},{5... | collective-permute-start | bytes 393224 | tf_op jit(solution)/shard_map/ppermute | solution.py:286
  13.5 0.9 slice_bitcast_fusion
  14.4 0.3 collective-permute-done.6.refs_10_
  14.7 0.0 collective-permute-done.3.refs_7_
  14.7 0.8 collective-permute-start.10
  15.5 0.3 collective-permute-start.7
  15.8 2.3 %collective-permute-done.8.refs_12_ = f32[32,1024]{1,0:T(8,128)S(1)} collective-permute-done((f32[32,1024]{1,0:T(8,128)S(1)}, f32[32,1024]{1,0:T(8,128)S(1)}, u32[]{:S(2)}, u32[]{:S(2)}) %collective-permute-start.8) | collective-permute-done | bytes 131104 | tf_op jit(solution)/shard_map/ppermute | solution.py:289
  18.2 1.9 %collective-permute-start.9 = (f32[32,1024]{1,0:T(8,128)S(1)}, f32[32,1024]{1,0:T(8,128)S(1)}, u32[]{:S(2)}, u32[]{:S(2)}) collective-permute-start(f32[32,1024]{1,0:T(8,128)S(1)} %collective-permute-done.8.refs_12_), channel_id=1, source_target_pairs={{0,4},{4,0},{8,12},{12,8},{16,20},{20,16},{24,28},{28,24},{1,5},{5... | collective-permute-start | bytes 393224 | tf_op jit(solution)/shard_map/ppermute | solution.py:286
  20.0 0.7 slice_bitcast_fusion.2
  20.8 7.4 %collective-permute-start.14 = (f32[33,4,128]{2,1,0:T(4,128)S(1)}, f32[33,4,128]{2,1,0:T(4,128)S(1)}, u32[]{:S(2)}, u32[]{:S(2)}) collective-permute-start(f32[33,4,128]{2,1,0:T(4,128)S(1)} %pad_maximum_fusion), channel_id=1, source_target_pairs={{0,1},{1,2},{2,3},{4,5},{5,6},{6,7},{8,9},{9,10},{10,11},{12,13},{... | collective-permute-start | bytes 202760 | tf_op jit(solution)/shard_map/ppermute | solution.py:320
  28.2 0.1 collective-permute-start.11
  28.3 1.4 %collective-permute-start.13 = (f32[32,1024]{1,0:T(8,128)S(1)}, f32[32,1024]{1,0:T(8,128)S(1)}, u32[]{:S(2)}, u32[]{:S(2)}) collective-permute-start(f32[32,1024]{1,0:T(8,128)S(1)} %collective-permute-done.12.refs_16_), channel_id=1, source_target_pairs={{0,4},{4,0},{8,12},{12,8},{16,20},{20,16},{24,28},{28,24},{1,5},{5... | collective-permute-start | bytes 393224 | tf_op jit(solution)/shard_map/ppermute | solution.py:286
  29.8 2.6 %collective-permute-start.15 = (f32[33,4,128]{2,1,0:T(4,128)S(1)}, f32[33,4,128]{2,1,0:T(4,128)S(1)}, u32[]{:S(2)}, u32[]{:S(2)}) collective-permute-start(f32[33,4,128]{2,1,0:T(4,128)S(1)} %pad_maximum_fusion.1), channel_id=1, source_target_pairs={{1,0},{2,1},{3,2},{5,4},{6,5},{7,6},{9,8},{10,9},{11,10},{13,12},{... | collective-permute-start | bytes 202760 | tf_op jit(solution)/shard_map/ppermute | solution.py:321
  32.4 0.1 add_convert_fusion.beside
  32.4 1.1 reshape.27.refs_21_
  33.5 1.9 %collective-permute-done.15.high_ref = f32[33,4,128]{2,1,0:T(4,128)S(1)} collective-permute-done((f32[33,4,128]{2,1,0:T(4,128)S(1)}, f32[33,4,128]{2,1,0:T(4,128)S(1)}, u32[]{:S(2)}, u32[]{:S(2)}) %collective-permute-start.15) | collective-permute-done | bytes 67616 | tf_op jit(solution)/shard_map/ppermute | solution.py:321
  35.4 0.9 copy-done
  36.3 1.0 shard_map.59
  37.3 0.0 copy-start.1
  37.4 2.2 %copy-done.1 = f32[32,64,512]{2,1,0:T(8,128)S(1)} copy-done((f32[32,64,512]{2,1,0:T(8,128)S(1)}, f32[32,64,512]{2,1,0:T(8,128)}, u32[]{:S(2)}) %copy-start.1) | copy-done | bytes 4194328
  39.5 12.2 %shard_map.60 = (f32[64,1024]{1,0:T(8,128)S(1)}, f32[2,64,512]{2,1,0:T(8,128)S(1)}, f32[2,64,512]{2,1,0:T(8,128)S(1)}) custom-call(s32[1]{0:T(128)} %bitcast.refs_0_, s32[16]{0:T(128)S(1)} %stack.76.refs_1_, f32[32,1024]{1,0:T(8,128)S(1)} %slice.31.refs_2_, f32[32,1024]{1,0:T(8,128)S(1)} %collective-permute-done.refs_3_, f32[32,1024]{1,0:T(8,128)S(1)} %slice.33.refs_4_, ...), custom_call_target="tpu_custom_call" | custom-call | flops 6442450944 | bytes 4194304 | tf_op jit(solution)/shard_map/pallas_call | solution.py:130
  51.8 1.9 %collective-permute-start.16 = (f32[2,64,512]{2,1,0:T(8,128)S(1)}, f32[2,64,512]{2,1,0:T(8,128)S(1)}, u32[]{:S(2)}, u32[]{:S(2)}) collective-permute-start(f32[2,64,512]{2,1,0:T(8,128)S(1)} %get-tuple-element.39.refs_3_), channel_id=1, source_target_pairs={{1,2},{2,1},{5,6},{6,5},{9,10},{10,9},{13,14},{14,13},{17,18},{18,... | collective-permute-start | bytes 786440 | tf_op jit(solution)/shard_map/ppermute | solution.py:334
  53.7 0.1 collective-permute-start.17
  53.8 6.0 %collective-permute-done.16.refs_5_ = f32[2,64,512]{2,1,0:T(8,128)S(1)} collective-permute-done((f32[2,64,512]{2,1,0:T(8,128)S(1)}, f32[2,64,512]{2,1,0:T(8,128)S(1)}, u32[]{:S(2)}, u32[]{:S(2)}) %collective-permute-start.16) | collective-permute-done | bytes 262176 | tf_op jit(solution)/shard_map/ppermute | solution.py:334
  59.8 0.3 shard_map.61.refs_20_.refs_2_
  60.1 0.4 collective-permute-start.22
  60.5 0.8 collective-permute-start.19
  61.3 1.5 %collective-permute-start.20 = (f32[32,1024]{1,0:T(8,128)S(1)}, f32[32,1024]{1,0:T(8,128)S(1)}, u32[]{:S(2)}, u32[]{:S(2)}) collective-permute-start(f32[32,1024]{1,0:T(8,128)S(1)} %get-tuple-element.55.refs_2_), channel_id=1, source_target_pairs={{0,8},{4,12},{8,16},{12,20},{16,24},{20,28},{24,0},{28,4},{1,9},{5... | collective-permute-start | bytes 393224 | tf_op jit(solution)/shard_map/ppermute | solution.py:289
  62.8 0.8 collective-permute-start.18
  63.6 2.2 %collective-permute-done.22.refs_8_ = f32[32,1024]{1,0:T(8,128)S(1)} collective-permute-done((f32[32,1024]{1,0:T(8,128)S(1)}, f32[32,1024]{1,0:T(8,128)S(1)}, u32[]{:S(2)}, u32[]{:S(2)}) %collective-permute-start.22) | collective-permute-done | bytes 131104 | tf_op jit(solution)/shard_map/ppermute | solution.py:289
  65.8 0.9 collective-permute-start.26
  66.7 1.3 %collective-permute-start.23 = (f32[32,1024]{1,0:T(8,128)S(1)}, f32[32,1024]{1,0:T(8,128)S(1)}, u32[]{:S(2)}, u32[]{:S(2)}) collective-permute-start(f32[32,1024]{1,0:T(8,128)S(1)} %collective-permute-done.22.refs_8_), channel_id=1, source_target_pairs={{0,4},{4,0},{8,12},{12,8},{16,20},{20,16},{24,28},{28,24},{1,5},{5... | collective-permute-start | bytes 393224 | tf_op jit(solution)/shard_map/ppermute | solution.py:286
  67.9 0.5 collective-permute-start.24
  68.4 2.2 %collective-permute-start.21 = (f32[32,1024]{1,0:T(8,128)S(1)}, f32[32,1024]{1,0:T(8,128)S(1)}, u32[]{:S(2)}, u32[]{:S(2)}) collective-permute-start(f32[32,1024]{1,0:T(8,128)S(1)} %collective-permute-done.20.refs_6_), channel_id=1, source_target_pairs={{0,4},{4,0},{8,12},{12,8},{16,20},{20,16},{24,28},{28,24},{1,5},{5... | collective-permute-start | bytes 393224 | tf_op jit(solution)/shard_map/ppermute | solution.py:286
  70.6 1.9 %collective-permute-done.26.refs_12_ = f32[32,1024]{1,0:T(8,128)S(1)} collective-permute-done((f32[32,1024]{1,0:T(8,128)S(1)}, f32[32,1024]{1,0:T(8,128)S(1)}, u32[]{:S(2)}, u32[]{:S(2)}) %collective-permute-start.26) | collective-permute-done | bytes 131104 | tf_op jit(solution)/shard_map/ppermute | solution.py:289
  72.5 1.2 %collective-permute-start.27 = (f32[32,1024]{1,0:T(8,128)S(1)}, f32[32,1024]{1,0:T(8,128)S(1)}, u32[]{:S(2)}, u32[]{:S(2)}) collective-permute-start(f32[32,1024]{1,0:T(8,128)S(1)} %collective-permute-done.26.refs_12_), channel_id=1, source_target_pairs={{0,4},{4,0},{8,12},{12,8},{16,20},{20,16},{24,28},{28,24},{1,5},{5... | collective-permute-start | bytes 393224 | tf_op jit(solution)/shard_map/ppermute | solution.py:286
  73.7 0.2 collective-permute-done.24.refs_10_
  73.9 0.7 collective-permute-start.28
  74.6 0.8 collective-permute-start.25
  75.4 3.5 %collective-permute-done.30.refs_16_ = f32[32,1024]{1,0:T(8,128)S(1)} collective-permute-done((f32[32,1024]{1,0:T(8,128)S(1)}, f32[32,1024]{1,0:T(8,128)S(1)}, u32[]{:S(2)}, u32[]{:S(2)}) %collective-permute-start.30) | collective-permute-done | bytes 131104 | tf_op jit(solution)/shard_map/ppermute | solution.py:289
  78.9 0.5 collective-permute-start.31
  79.4 1.5 %collective-permute-done.28.refs_14_ = f32[32,1024]{1,0:T(8,128)S(1)} collective-permute-done((f32[32,1024]{1,0:T(8,128)S(1)}, f32[32,1024]{1,0:T(8,128)S(1)}, u32[]{:S(2)}, u32[]{:S(2)}) %collective-permute-start.28) | collective-permute-done | bytes 131104 | tf_op jit(solution)/shard_map/ppermute | solution.py:289
  80.9 0.9 collective-permute-start.29
  81.8 1.0 collective-permute-done.31.refs_17_
  82.7 3.1 %collective-permute-done.29.refs_15_ = f32[32,1024]{1,0:T(8,128)S(1)} collective-permute-done((f32[32,1024]{1,0:T(8,128)S(1)}, f32[32,1024]{1,0:T(8,128)S(1)}, u32[]{:S(2)}, u32[]{:S(2)}) %collective-permute-start.29) | collective-permute-done | bytes 131104 | tf_op jit(solution)/shard_map/ppermute | solution.py:286
  85.8 12.3 %shard_map.62 = (f32[64,1024]{1,0:T(8,128)S(1)}, f32[2,64,512]{2,1,0:T(8,128)S(1)}, f32[2,64,512]{2,1,0:T(8,128)S(1)}) custom-call(s32[1]{0:T(128)} %bitcast.refs_0_, s32[16]{0:T(128)S(1)} %stack.76.refs_1_, f32[32,1024]{1,0:T(8,128)S(1)} %get-tuple-element.55.refs_2_, f32[32,1024]{1,0:T(8,128)S(1)} %collective-permute-done.18.refs_3_, ...), custom_call_target="tpu_custom_call" | custom-call | flops 6442450944 | bytes 4194304 | tf_op jit(solution)/shard_map/pallas_call | solution.py:130
  98.1 5.7 %collective-permute-start.32 = (f32[2,64,512]{2,1,0:T(8,128)S(1)}, f32[2,64,512]{2,1,0:T(8,128)S(1)}, u32[]{:S(2)}, u32[]{:S(2)}) collective-permute-start(f32[2,64,512]{2,1,0:T(8,128)S(1)} %get-tuple-element.50.refs_3_), channel_id=1, source_target_pairs={{1,2},{2,1},{5,6},{6,5},{9,10},{10,9},{13,14},{14,13},{17,18},{18,... | collective-permute-start | bytes 786440 | tf_op jit(solution)/shard_map/ppermute | solution.py:334
  103.8 0.1 collective-permute-start.33
  103.9 4.0 %collective-permute-done.32.refs_5_ = f32[2,64,512]{2,1,0:T(8,128)S(1)} collective-permute-done((f32[2,64,512]{2,1,0:T(8,128)S(1)}, f32[2,64,512]{2,1,0:T(8,128)S(1)}, u32[]{:S(2)}, u32[]{:S(2)}) %collective-permute-start.32) | collective-permute-done | bytes 262176 | tf_op jit(solution)/shard_map/ppermute | solution.py:334
  107.9 1.3 %shard_map.63 = (f32[64,8,128]{2,1,0:T(8,128)}, f32[64,8,128]{2,1,0:T(8,128)}) custom-call(s32[1]{0:T(128)} %bitcast.refs_0_, f32[64,1024]{1,0:T(8,128)S(1)} %get-tuple-element.49.refs_1_, f32[64,1024]{1,0:T(8,128)S(1)} %shard_map.61.refs_20_.refs_2_, f32[2,64,512]{2,1,0:T(8,128)S(1)} %get-tuple-element.50.refs_3_, ...), custom_call_target="tpu_custom_call" | custom-call | flops 2621440 | tf_op jit(solution)/shard_map/pallas_call | solution.py:203
  (27 shorter events, 0.1 us)
Async XLA Ops:
  1.7 7.4 %collective-permute-start.2 = (f32[32,1024]{1,0:T(8,128)S(1)}, f32[32,1024]{1,0:T(8,128)S(1)}, u32[]{:S(2)}, u32[]{:S(2)}) collective-permute-start(f32[32,1024]{1,0:T(8,128)S(1)} %slice.31.refs_2_), channel_id=1, source_target_pairs={{0,8},{4,12},{8,16},{12,20},{16,24},{20,28},{24,0},{28,4},{1,9},{5... | collective-permute-start | bytes 393224 | tf_op jit(solution)/shard_map/ppermute | solution.py:289
  3.9 5.3 %collective-permute-start = (f32[32,1024]{1,0:T(8,128)S(1)}, f32[32,1024]{1,0:T(8,128)S(1)}, u32[]{:S(2)}, u32[]{:S(2)}) collective-permute-start(f32[32,1024]{1,0:T(8,128)S(1)} %slice.31.refs_2_), channel_id=1, source_target_pairs={{0,4},{4,0},{8,12},{12,8},{16,20},{20,16},{24,28},{28,24},{1,5},{5... | collective-permute-start | bytes 393224 | tf_op jit(solution)/shard_map/ppermute | solution.py:286
  5.2 5.9 %collective-permute-start.4 = (f32[32,1024]{1,0:T(8,128)S(1)}, f32[32,1024]{1,0:T(8,128)S(1)}, u32[]{:S(2)}, u32[]{:S(2)}) collective-permute-start(f32[32,1024]{1,0:T(8,128)S(1)} %slice.33.refs_4_), channel_id=1, source_target_pairs={{0,8},{4,12},{8,16},{12,20},{16,24},{20,28},{24,0},{28,4},{1,9},{5... | collective-permute-start | bytes 393224 | tf_op jit(solution)/shard_map/ppermute | solution.py:289
  6.5 4.5 %collective-permute-start.1 = (f32[32,1024]{1,0:T(8,128)S(1)}, f32[32,1024]{1,0:T(8,128)S(1)}, u32[]{:S(2)}, u32[]{:S(2)}) collective-permute-start(f32[32,1024]{1,0:T(8,128)S(1)} %slice.33.refs_4_), channel_id=1, source_target_pairs={{0,4},{4,0},{8,12},{12,8},{16,20},{20,16},{24,28},{28,24},{1,5},{5... | collective-permute-start | bytes 393224 | tf_op jit(solution)/shard_map/ppermute | solution.py:286
  9.1 5.6 %collective-permute-start.6 = (f32[32,1024]{1,0:T(8,128)S(1)}, f32[32,1024]{1,0:T(8,128)S(1)}, u32[]{:S(2)}, u32[]{:S(2)}) collective-permute-start(f32[32,1024]{1,0:T(8,128)S(1)} %collective-permute-done.2.refs_6_), channel_id=1, source_target_pairs={{0,8},{4,12},{8,16},{12,20},{16,24},{20,28},{24,0},{28,4},{1,9},{5... | collective-permute-start | bytes 393224 | tf_op jit(solution)/shard_map/ppermute | solution.py:289
  9.3 5.4 %collective-permute-start.3 = (f32[32,1024]{1,0:T(8,128)S(1)}, f32[32,1024]{1,0:T(8,128)S(1)}, u32[]{:S(2)}, u32[]{:S(2)}) collective-permute-start(f32[32,1024]{1,0:T(8,128)S(1)} %collective-permute-done.2.refs_6_), channel_id=1, source_target_pairs={{0,4},{4,0},{8,12},{12,8},{16,20},{20,16},{24,28},{28,24},{1,5},{5... | collective-permute-start | bytes 393224 | tf_op jit(solution)/shard_map/ppermute | solution.py:286
  11.1 7.1 %collective-permute-start.8 = (f32[32,1024]{1,0:T(8,128)S(1)}, f32[32,1024]{1,0:T(8,128)S(1)}, u32[]{:S(2)}, u32[]{:S(2)}) collective-permute-start(f32[32,1024]{1,0:T(8,128)S(1)} %collective-permute-done.4.refs_8_), channel_id=1, source_target_pairs={{0,8},{4,12},{8,16},{12,20},{16,24},{20,28},{24,0},{28,4},{1,9},{5... | collective-permute-start | bytes 393224 | tf_op jit(solution)/shard_map/ppermute | solution.py:289
  12.1 6.1 %collective-permute-start.5 = (f32[32,1024]{1,0:T(8,128)S(1)}, f32[32,1024]{1,0:T(8,128)S(1)}, u32[]{:S(2)}, u32[]{:S(2)}) collective-permute-start(f32[32,1024]{1,0:T(8,128)S(1)} %collective-permute-done.4.refs_8_), channel_id=1, source_target_pairs={{0,4},{4,0},{8,12},{12,8},{16,20},{20,16},{24,28},{28,24},{1,5},{5... | collective-permute-start | bytes 393224 | tf_op jit(solution)/shard_map/ppermute | solution.py:286
  14.7 13.5 %collective-permute-start.10 = (f32[32,1024]{1,0:T(8,128)S(1)}, f32[32,1024]{1,0:T(8,128)S(1)}, u32[]{:S(2)}, u32[]{:S(2)}) collective-permute-start(f32[32,1024]{1,0:T(8,128)S(1)} %collective-permute-done.6.refs_10_), channel_id=1, source_target_pairs={{0,8},{4,12},{8,16},{12,20},{16,24},{20,28},{24,0},{28,4},{1,9},{5... | collective-permute-start | bytes 393224 | tf_op jit(solution)/shard_map/ppermute | solution.py:289
  15.5 12.7 %collective-permute-start.7 = (f32[32,1024]{1,0:T(8,128)S(1)}, f32[32,1024]{1,0:T(8,128)S(1)}, u32[]{:S(2)}, u32[]{:S(2)}) collective-permute-start(f32[32,1024]{1,0:T(8,128)S(1)} %collective-permute-done.6.refs_10_), channel_id=1, source_target_pairs={{0,4},{4,0},{8,12},{12,8},{16,20},{20,16},{24,28},{28,24},{1,5},{5... | collective-permute-start | bytes 393224 | tf_op jit(solution)/shard_map/ppermute | solution.py:286
  18.2 10.1 %collective-permute-start.12 = (f32[32,1024]{1,0:T(8,128)S(1)}, f32[32,1024]{1,0:T(8,128)S(1)}, u32[]{:S(2)}, u32[]{:S(2)}) collective-permute-start(f32[32,1024]{1,0:T(8,128)S(1)} %collective-permute-done.8.refs_12_), channel_id=1, source_target_pairs={{0,8},{4,12},{8,16},{12,20},{16,24},{20,28},{24,0},{28,4},{1,9},{5... | collective-permute-start | bytes 393224 | tf_op jit(solution)/shard_map/ppermute | solution.py:289
  18.2 10.1 %collective-permute-start.9 = (f32[32,1024]{1,0:T(8,128)S(1)}, f32[32,1024]{1,0:T(8,128)S(1)}, u32[]{:S(2)}, u32[]{:S(2)}) collective-permute-start(f32[32,1024]{1,0:T(8,128)S(1)} %collective-permute-done.8.refs_12_), channel_id=1, source_target_pairs={{0,4},{4,0},{8,12},{12,8},{16,20},{20,16},{24,28},{28,24},{1,5},{5... | collective-permute-start | bytes 393224 | tf_op jit(solution)/shard_map/ppermute | solution.py:286
  20.8 12.7 %collective-permute-start.14 = (f32[33,4,128]{2,1,0:T(4,128)S(1)}, f32[33,4,128]{2,1,0:T(4,128)S(1)}, u32[]{:S(2)}, u32[]{:S(2)}) collective-permute-start(f32[33,4,128]{2,1,0:T(4,128)S(1)} %pad_maximum_fusion), channel_id=1, source_target_pairs={{0,1},{1,2},{2,3},{4,5},{5,6},{6,7},{8,9},{9,10},{10,11},{12,13},{... | collective-permute-start | bytes 202760 | tf_op jit(solution)/shard_map/ppermute | solution.py:320
  28.2 9.1 %collective-permute-start.11 = (f32[32,1024]{1,0:T(8,128)S(1)}, f32[32,1024]{1,0:T(8,128)S(1)}, u32[]{:S(2)}, u32[]{:S(2)}) collective-permute-start(f32[32,1024]{1,0:T(8,128)S(1)} %collective-permute-done.10.refs_14_), channel_id=1, source_target_pairs={{0,4},{4,0},{8,12},{12,8},{16,20},{20,16},{24,28},{28,24},{1,5},{5... | collective-permute-start | bytes 393224 | tf_op jit(solution)/shard_map/ppermute | solution.py:286
  28.3 9.0 %collective-permute-start.13 = (f32[32,1024]{1,0:T(8,128)S(1)}, f32[32,1024]{1,0:T(8,128)S(1)}, u32[]{:S(2)}, u32[]{:S(2)}) collective-permute-start(f32[32,1024]{1,0:T(8,128)S(1)} %collective-permute-done.12.refs_16_), channel_id=1, source_target_pairs={{0,4},{4,0},{8,12},{12,8},{16,20},{20,16},{24,28},{28,24},{1,5},{5... | collective-permute-start | bytes 393224 | tf_op jit(solution)/shard_map/ppermute | solution.py:286
  29.8 5.6 %collective-permute-start.15 = (f32[33,4,128]{2,1,0:T(4,128)S(1)}, f32[33,4,128]{2,1,0:T(4,128)S(1)}, u32[]{:S(2)}, u32[]{:S(2)}) collective-permute-start(f32[33,4,128]{2,1,0:T(4,128)S(1)} %pad_maximum_fusion.1), channel_id=1, source_target_pairs={{1,0},{2,1},{3,2},{5,4},{6,5},{7,6},{9,8},{10,9},{11,10},{13,12},{... | collective-permute-start | bytes 202760 | tf_op jit(solution)/shard_map/ppermute | solution.py:321
  35.4 0.9 copy-start
  37.3 2.2 %copy-start.1 = (f32[32,64,512]{2,1,0:T(8,128)S(1)}, f32[32,64,512]{2,1,0:T(8,128)}, u32[]{:S(2)}) copy-start(f32[32,64,512]{2,1,0:T(8,128)} %refs_18_.3) | copy-start | bytes 12582916
  39.5 46.3 %copy-start.2 = (f32[32,64,512]{2,1,0:T(8,128)S(1)}, f32[32,64,512]{2,1,0:T(8,128)}, u32[]{:S(2)}) copy-start(f32[32,64,512]{2,1,0:T(8,128)} %refs_18_.3) | copy-start | bytes 12582916
  51.8 8.0 %collective-permute-start.16 = (f32[2,64,512]{2,1,0:T(8,128)S(1)}, f32[2,64,512]{2,1,0:T(8,128)S(1)}, u32[]{:S(2)}, u32[]{:S(2)}) collective-permute-start(f32[2,64,512]{2,1,0:T(8,128)S(1)} %get-tuple-element.39.refs_3_), channel_id=1, source_target_pairs={{1,2},{2,1},{5,6},{6,5},{9,10},{10,9},{13,14},{14,13},{17,18},{18,... | collective-permute-start | bytes 786440 | tf_op jit(solution)/shard_map/ppermute | solution.py:334
  53.7 6.1 %collective-permute-start.17 = (f32[2,64,512]{2,1,0:T(8,128)S(1)}, f32[2,64,512]{2,1,0:T(8,128)S(1)}, u32[]{:S(2)}, u32[]{:S(2)}) collective-permute-start(f32[2,64,512]{2,1,0:T(8,128)S(1)} %get-tuple-element.40.refs_4_), channel_id=1, source_target_pairs={{0,1},{2,3},{1,0},{3,2},{4,5},{6,7},{5,4},{7,6},{8,9},{10,11},{9,8... | collective-permute-start | bytes 786440 | tf_op jit(solution)/shard_map/ppermute | solution.py:335
  60.1 5.7 %collective-permute-start.22 = (f32[32,1024]{1,0:T(8,128)S(1)}, f32[32,1024]{1,0:T(8,128)S(1)}, u32[]{:S(2)}, u32[]{:S(2)}) collective-permute-start(f32[32,1024]{1,0:T(8,128)S(1)} %get-tuple-element.54.refs_4_), channel_id=1, source_target_pairs={{0,8},{4,12},{8,16},{12,20},{16,24},{20,28},{24,0},{28,4},{1,9},{5... | collective-permute-start | bytes 393224 | tf_op jit(solution)/shard_map/ppermute | solution.py:289
  60.5 5.3 %collective-permute-start.19 = (f32[32,1024]{1,0:T(8,128)S(1)}, f32[32,1024]{1,0:T(8,128)S(1)}, u32[]{:S(2)}, u32[]{:S(2)}) collective-permute-start(f32[32,1024]{1,0:T(8,128)S(1)} %get-tuple-element.54.refs_4_), channel_id=1, source_target_pairs={{0,4},{4,0},{8,12},{12,8},{16,20},{20,16},{24,28},{28,24},{1,5},{5... | collective-permute-start | bytes 393224 | tf_op jit(solution)/shard_map/ppermute | solution.py:286
  61.3 6.6 %collective-permute-start.20 = (f32[32,1024]{1,0:T(8,128)S(1)}, f32[32,1024]{1,0:T(8,128)S(1)}, u32[]{:S(2)}, u32[]{:S(2)}) collective-permute-start(f32[32,1024]{1,0:T(8,128)S(1)} %get-tuple-element.55.refs_2_), channel_id=1, source_target_pairs={{0,8},{4,12},{8,16},{12,20},{16,24},{20,28},{24,0},{28,4},{1,9},{5... | collective-permute-start | bytes 393224 | tf_op jit(solution)/shard_map/ppermute | solution.py:289
  62.8 5.1 %collective-permute-start.18 = (f32[32,1024]{1,0:T(8,128)S(1)}, f32[32,1024]{1,0:T(8,128)S(1)}, u32[]{:S(2)}, u32[]{:S(2)}) collective-permute-start(f32[32,1024]{1,0:T(8,128)S(1)} %get-tuple-element.55.refs_2_), channel_id=1, source_target_pairs={{0,4},{4,0},{8,12},{12,8},{16,20},{20,16},{24,28},{28,24},{1,5},{5... | collective-permute-start | bytes 393224 | tf_op jit(solution)/shard_map/ppermute | solution.py:286
  65.8 6.7 %collective-permute-start.26 = (f32[32,1024]{1,0:T(8,128)S(1)}, f32[32,1024]{1,0:T(8,128)S(1)}, u32[]{:S(2)}, u32[]{:S(2)}) collective-permute-start(f32[32,1024]{1,0:T(8,128)S(1)} %collective-permute-done.22.refs_8_), channel_id=1, source_target_pairs={{0,8},{4,12},{8,16},{12,20},{16,24},{20,28},{24,0},{28,4},{1,9},{5... | collective-permute-start | bytes 393224 | tf_op jit(solution)/shard_map/ppermute | solution.py:289
  66.7 5.8 %collective-permute-start.23 = (f32[32,1024]{1,0:T(8,128)S(1)}, f32[32,1024]{1,0:T(8,128)S(1)}, u32[]{:S(2)}, u32[]{:S(2)}) collective-permute-start(f32[32,1024]{1,0:T(8,128)S(1)} %collective-permute-done.22.refs_8_), channel_id=1, source_target_pairs={{0,4},{4,0},{8,12},{12,8},{16,20},{20,16},{24,28},{28,24},{1,5},{5... | collective-permute-start | bytes 393224 | tf_op jit(solution)/shard_map/ppermute | solution.py:286
  67.9 5.9 %collective-permute-start.24 = (f32[32,1024]{1,0:T(8,128)S(1)}, f32[32,1024]{1,0:T(8,128)S(1)}, u32[]{:S(2)}, u32[]{:S(2)}) collective-permute-start(f32[32,1024]{1,0:T(8,128)S(1)} %collective-permute-done.20.refs_6_), channel_id=1, source_target_pairs={{0,8},{4,12},{8,16},{12,20},{16,24},{20,28},{24,0},{28,4},{1,9},{5... | collective-permute-start | bytes 393224 | tf_op jit(solution)/shard_map/ppermute | solution.py:289
  68.4 5.5 %collective-permute-start.21 = (f32[32,1024]{1,0:T(8,128)S(1)}, f32[32,1024]{1,0:T(8,128)S(1)}, u32[]{:S(2)}, u32[]{:S(2)}) collective-permute-start(f32[32,1024]{1,0:T(8,128)S(1)} %collective-permute-done.20.refs_6_), channel_id=1, source_target_pairs={{0,4},{4,0},{8,12},{12,8},{16,20},{20,16},{24,28},{28,24},{1,5},{5... | collective-permute-start | bytes 393224 | tf_op jit(solution)/shard_map/ppermute | solution.py:286
  72.5 6.4 %collective-permute-start.30 = (f32[32,1024]{1,0:T(8,128)S(1)}, f32[32,1024]{1,0:T(8,128)S(1)}, u32[]{:S(2)}, u32[]{:S(2)}) collective-permute-start(f32[32,1024]{1,0:T(8,128)S(1)} %collective-permute-done.26.refs_12_), channel_id=1, source_target_pairs={{0,8},{4,12},{8,16},{12,20},{16,24},{20,28},{24,0},{28,4},{1,9},{5... | collective-permute-start | bytes 393224 | tf_op jit(solution)/shard_map/ppermute | solution.py:289
  72.5 6.4 %collective-permute-start.27 = (f32[32,1024]{1,0:T(8,128)S(1)}, f32[32,1024]{1,0:T(8,128)S(1)}, u32[]{:S(2)}, u32[]{:S(2)}) collective-permute-start(f32[32,1024]{1,0:T(8,128)S(1)} %collective-permute-done.26.refs_12_), channel_id=1, source_target_pairs={{0,4},{4,0},{8,12},{12,8},{16,20},{20,16},{24,28},{28,24},{1,5},{5... | collective-permute-start | bytes 393224 | tf_op jit(solution)/shard_map/ppermute | solution.py:286
  73.9 7.0 %collective-permute-start.28 = (f32[32,1024]{1,0:T(8,128)S(1)}, f32[32,1024]{1,0:T(8,128)S(1)}, u32[]{:S(2)}, u32[]{:S(2)}) collective-permute-start(f32[32,1024]{1,0:T(8,128)S(1)} %collective-permute-done.24.refs_10_), channel_id=1, source_target_pairs={{0,8},{4,12},{8,16},{12,20},{16,24},{20,28},{24,0},{28,4},{1,9},{5... | collective-permute-start | bytes 393224 | tf_op jit(solution)/shard_map/ppermute | solution.py:289
  74.6 6.3 %collective-permute-start.25 = (f32[32,1024]{1,0:T(8,128)S(1)}, f32[32,1024]{1,0:T(8,128)S(1)}, u32[]{:S(2)}, u32[]{:S(2)}) collective-permute-start(f32[32,1024]{1,0:T(8,128)S(1)} %collective-permute-done.24.refs_10_), channel_id=1, source_target_pairs={{0,4},{4,0},{8,12},{12,8},{16,20},{20,16},{24,28},{28,24},{1,5},{5... | collective-permute-start | bytes 393224 | tf_op jit(solution)/shard_map/ppermute | solution.py:286
  78.9 3.8 %collective-permute-start.31 = (f32[32,1024]{1,0:T(8,128)S(1)}, f32[32,1024]{1,0:T(8,128)S(1)}, u32[]{:S(2)}, u32[]{:S(2)}) collective-permute-start(f32[32,1024]{1,0:T(8,128)S(1)} %collective-permute-done.30.refs_16_), channel_id=1, source_target_pairs={{0,4},{4,0},{8,12},{12,8},{16,20},{20,16},{24,28},{28,24},{1,5},{5... | collective-permute-start | bytes 393224 | tf_op jit(solution)/shard_map/ppermute | solution.py:286
  80.9 4.9 %collective-permute-start.29 = (f32[32,1024]{1,0:T(8,128)S(1)}, f32[32,1024]{1,0:T(8,128)S(1)}, u32[]{:S(2)}, u32[]{:S(2)}) collective-permute-start(f32[32,1024]{1,0:T(8,128)S(1)} %collective-permute-done.28.refs_14_), channel_id=1, source_target_pairs={{0,4},{4,0},{8,12},{12,8},{16,20},{20,16},{24,28},{28,24},{1,5},{5... | collective-permute-start | bytes 393224 | tf_op jit(solution)/shard_map/ppermute | solution.py:286
  98.1 9.7 %collective-permute-start.32 = (f32[2,64,512]{2,1,0:T(8,128)S(1)}, f32[2,64,512]{2,1,0:T(8,128)S(1)}, u32[]{:S(2)}, u32[]{:S(2)}) collective-permute-start(f32[2,64,512]{2,1,0:T(8,128)S(1)} %get-tuple-element.50.refs_3_), channel_id=1, source_target_pairs={{1,2},{2,1},{5,6},{6,5},{9,10},{10,9},{13,14},{14,13},{17,18},{18,... | collective-permute-start | bytes 786440 | tf_op jit(solution)/shard_map/ppermute | solution.py:334
  103.8 4.0 %collective-permute-start.33 = (f32[2,64,512]{2,1,0:T(8,128)S(1)}, f32[2,64,512]{2,1,0:T(8,128)S(1)}, u32[]{:S(2)}, u32[]{:S(2)}) collective-permute-start(f32[2,64,512]{2,1,0:T(8,128)S(1)} %get-tuple-element.51.refs_4_), channel_id=1, source_target_pairs={{0,1},{2,3},{1,0},{3,2},{4,5},{6,7},{5,4},{7,6},{8,9},{10,11},{9,8... | collective-permute-start | bytes 786440 | tf_op jit(solution)/shard_map/ppermute | solution.py:335

commit v2 on v1

--- a/solution.py
+++ b/solution.py
@@ -125,7 +125,7 @@
     rows, lanes_all = press.shape
     cells = lanes_all // planes
     terms, _, modes = c.shape
-    chunks = max(1, terms * rows // 256)
+    chunks = max(1, terms * rows // 512)
     sent = jax.ShapeDtypeStruct((2, rows, cells), jnp.float32)
     return pl.pallas_call(
         lambda *refs: mix_kernel(planes, len(blocks), *refs),

time: 110 us -> 108 us (0.982)
  waiting for transfers between devices: 29.5 us -> 31.7 us
  starting transfers between devices: 43.5 us -> 41.4 us
  Pallas kernels: 27.1 us -> 25.5 us
    ppermute x12, waiting for transfers between devices: 13.6 us -> 16 us  [gathered(): current[h] = after(lax.ppermute(sent[h], 'mode', ring), block)]
    ppermute x16, starting transfers between devices: 16.3 us -> 14.7 us  [gathered(): block = lax.ppermute(block, 'mode', turned)]
    pallas_call x2, Pallas kernels: 24.5 us -> 22.9 us  [mix(): pl.pallas_call(lambda *refs: mix_kernel(planes, len(blocks), *refs), in_s...]
where the time goes in v2:
time: 108 us
  starting transfers between devices  41.4 us (38%)
  waiting for transfers between devices  31.7 us (29%)
  Pallas kernels  25.5 us (24%)
  local copies, waits for them, and re-layouts  7.99 us (7%)
    pallas_call x2, Pallas kernels, mix(): pl.pallas_call(lambda *refs: mix_kernel(planes, len(blocks), *refs), in_s...  22.9 us
    ppermute x12, waiting for transfers between devices, gathered(): current[h] = after(lax.ppermute(sent[h], 'mode', ring), block)  16 us
    ppermute x16, starting transfers between devices, gathered(): block = lax.ppermute(block, 'mode', turned)  14.7 us
    ppermute x2, waiting for transfers between devices, on_device(): odd_in = lax.ppermute(odd_own, 'space', swap_odd)  9.47 us
    ppermute x12, starting transfers between devices, gathered(): current[h] = after(lax.ppermute(sent[h], 'mode', ring), block)  9.21 us
    ppermute x1, starting transfers between devices, on_device(): lax.ppermute(jnp.concatenate([coefficients[:, planes - 1], coefficients[:...  7.43 us
    ppermute x2, starting transfers between devices, on_device(): odd_in = lax.ppermute(odd_own, 'space', swap_odd)  7.39 us
    ppermute x16, waiting for transfers between devices, gathered(): block = lax.ppermute(block, 'mode', turned)  4.34 us
  transfers between devices with their start and end apart: 34, of which 14 were waited for; matrix products, arithmetic and copies ran while one was open for 4% of the time, Pallas kernels for 1%

profile of v2, /device:TPU:1, one launch (start us, length us, event | category | flops | bytes accessed | tf_op | source)
XLA Modules:
  0.0 107.6 jit_solution(11050786647329896426)
XLA Ops:
  0.6 1.0 fusion.1
  1.6 0.1 slice.31.refs_2_
  1.7 2.2 %collective-permute-start.2 = (f32[32,1024]{1,0:T(8,128)S(1)}, f32[32,1024]{1,0:T(8,128)S(1)}, u32[]{:S(2)}, u32[]{:S(2)}) collective-permute-start(f32[32,1024]{1,0:T(8,128)S(1)} %slice.31.refs_2_), channel_id=1, source_target_pairs={{0,8},{4,12},{8,16},{12,20},{16,24},{20,28},{24,0},{28,4},{1,9},{5... | collective-permute-start | bytes 393224 | tf_op jit(solution)/shard_map/ppermute | solution.py:289
  3.9 1.2 %collective-permute-start = (f32[32,1024]{1,0:T(8,128)S(1)}, f32[32,1024]{1,0:T(8,128)S(1)}, u32[]{:S(2)}, u32[]{:S(2)}) collective-permute-start(f32[32,1024]{1,0:T(8,128)S(1)} %slice.31.refs_2_), channel_id=1, source_target_pairs={{0,4},{4,0},{8,12},{12,8},{16,20},{20,16},{24,28},{28,24},{1,5},{5... | collective-permute-start | bytes 393224 | tf_op jit(solution)/shard_map/ppermute | solution.py:286
  5.1 0.1 slice.33.refs_4_
  5.2 1.3 %collective-permute-start.4 = (f32[32,1024]{1,0:T(8,128)S(1)}, f32[32,1024]{1,0:T(8,128)S(1)}, u32[]{:S(2)}, u32[]{:S(2)}) collective-permute-start(f32[32,1024]{1,0:T(8,128)S(1)} %slice.33.refs_4_), channel_id=1, source_target_pairs={{0,8},{4,12},{8,16},{12,20},{16,24},{20,28},{24,0},{28,4},{1,9},{5... | collective-permute-start | bytes 393224 | tf_op jit(solution)/shard_map/ppermute | solution.py:289
  6.5 0.2 collective-permute-start.1
  6.7 1.1 reshape.26.refs_20_.refs_2_
  7.8 0.1 stack.76.refs_1_
  7.9 1.2 %collective-permute-done.2.refs_6_ = f32[32,1024]{1,0:T(8,128)S(1)} collective-permute-done((f32[32,1024]{1,0:T(8,128)S(1)}, f32[32,1024]{1,0:T(8,128)S(1)}, u32[]{:S(2)}, u32[]{:S(2)}) %collective-permute-start.2) | collective-permute-done | bytes 131104 | tf_op jit(solution)/shard_map/ppermute | solution.py:289
  9.1 0.0 collective-permute-done.refs_3_
  9.1 0.2 collective-permute-start.6
  9.3 1.2 %collective-permute-start.3 = (f32[32,1024]{1,0:T(8,128)S(1)}, f32[32,1024]{1,0:T(8,128)S(1)}, u32[]{:S(2)}, u32[]{:S(2)}) collective-permute-start(f32[32,1024]{1,0:T(8,128)S(1)} %collective-permute-done.2.refs_6_), channel_id=1, source_target_pairs={{0,4},{4,0},{8,12},{12,8},{16,20},{20,16},{24,28},{28,24},{1,5},{5... | collective-permute-start | bytes 393224 | tf_op jit(solution)/shard_map/ppermute | solution.py:286
  10.5 0.5 collective-permute-done.4.refs_8_
  11.1 0.0 collective-permute-done.1.refs_5_
  11.1 1.0 collective-permute-start.8
  12.1 1.5 %collective-permute-start.5 = (f32[32,1024]{1,0:T(8,128)S(1)}, f32[32,1024]{1,0:T(8,128)S(1)}, u32[]{:S(2)}, u32[]{:S(2)}) collective-permute-start(f32[32,1024]{1,0:T(8,128)S(1)} %collective-permute-done.4.refs_8_), channel_id=1, source_target_pairs={{0,4},{4,0},{8,12},{12,8},{16,20},{20,16},{24,28},{28,24},{1,5},{5... | collective-permute-start | bytes 393224 | tf_op jit(solution)/shard_map/ppermute | solution.py:286
  13.5 0.9 slice_bitcast_fusion
  14.4 0.3 collective-permute-done.6.refs_10_
  14.7 0.8 collective-permute-start.10
  15.5 0.3 collective-permute-start.7
  15.8 2.3 %collective-permute-done.8.refs_12_ = f32[32,1024]{1,0:T(8,128)S(1)} collective-permute-done((f32[32,1024]{1,0:T(8,128)S(1)}, f32[32,1024]{1,0:T(8,128)S(1)}, u32[]{:S(2)}, u32[]{:S(2)}) %collective-permute-start.8) | collective-permute-done | bytes 131104 | tf_op jit(solution)/shard_map/ppermute | solution.py:289
  18.2 1.9 %collective-permute-start.9 = (f32[32,1024]{1,0:T(8,128)S(1)}, f32[32,1024]{1,0:T(8,128)S(1)}, u32[]{:S(2)}, u32[]{:S(2)}) collective-permute-start(f32[32,1024]{1,0:T(8,128)S(1)} %collective-permute-done.8.refs_12_), channel_id=1, source_target_pairs={{0,4},{4,0},{8,12},{12,8},{16,20},{20,16},{24,28},{28,24},{1,5},{5... | collective-permute-start | bytes 393224 | tf_op jit(solution)/shard_map/ppermute | solution.py:286
  20.0 0.7 slice_bitcast_fusion.2
  20.8 7.4 %collective-permute-start.14 = (f32[33,4,128]{2,1,0:T(4,128)S(1)}, f32[33,4,128]{2,1,0:T(4,128)S(1)}, u32[]{:S(2)}, u32[]{:S(2)}) collective-permute-start(f32[33,4,128]{2,1,0:T(4,128)S(1)} %pad_maximum_fusion), channel_id=1, source_target_pairs={{0,1},{1,2},{2,3},{4,5},{5,6},{6,7},{8,9},{9,10},{10,11},{12,13},{... | collective-permute-start | bytes 202760 | tf_op jit(solution)/shard_map/ppermute | solution.py:320
  28.2 0.1 collective-permute-start.11
  28.3 1.4 %collective-permute-start.13 = (f32[32,1024]{1,0:T(8,128)S(1)}, f32[32,1024]{1,0:T(8,128)S(1)}, u32[]{:S(2)}, u32[]{:S(2)}) collective-permute-start(f32[32,1024]{1,0:T(8,128)S(1)} %collective-permute-done.12.refs_16_), channel_id=1, source_target_pairs={{0,4},{4,0},{8,12},{12,8},{16,20},{20,16},{24,28},{28,24},{1,5},{5... | collective-permute-start | bytes 393224 | tf_op jit(solution)/shard_map/ppermute | solution.py:286
  29.8 2.6 %collective-permute-start.15 = (f32[33,4,128]{2,1,0:T(4,128)S(1)}, f32[33,4,128]{2,1,0:T(4,128)S(1)}, u32[]{:S(2)}, u32[]{:S(2)}) collective-permute-start(f32[33,4,128]{2,1,0:T(4,128)S(1)} %pad_maximum_fusion.1), channel_id=1, source_target_pairs={{1,0},{2,1},{3,2},{5,4},{6,5},{7,6},{9,8},{10,9},{11,10},{13,12},{... | collective-permute-start | bytes 202760 | tf_op jit(solution)/shard_map/ppermute | solution.py:321
  32.4 0.1 add_convert_fusion.beside
  32.4 1.1 reshape.27.refs_21_
  33.5 1.9 %collective-permute-done.15.high_ref = f32[33,4,128]{2,1,0:T(4,128)S(1)} collective-permute-done((f32[33,4,128]{2,1,0:T(4,128)S(1)}, f32[33,4,128]{2,1,0:T(4,128)S(1)}, u32[]{:S(2)}, u32[]{:S(2)}) %collective-permute-start.15) | collective-permute-done | bytes 67616 | tf_op jit(solution)/shard_map/ppermute | solution.py:321
  35.4 0.9 copy-done
  36.3 1.0 shard_map.59
  37.3 0.0 copy-start.1
  37.4 2.2 %copy-done.1 = f32[32,64,512]{2,1,0:T(8,128)S(1)} copy-done((f32[32,64,512]{2,1,0:T(8,128)S(1)}, f32[32,64,512]{2,1,0:T(8,128)}, u32[]{:S(2)}) %copy-start.1) | copy-done | bytes 4194328
  39.5 11.4 %shard_map.60 = (f32[64,1024]{1,0:T(8,128)S(1)}, f32[2,64,512]{2,1,0:T(8,128)S(1)}, f32[2,64,512]{2,1,0:T(8,128)S(1)}) custom-call(s32[1]{0:T(128)} %bitcast.refs_0_, s32[16]{0:T(128)S(1)} %stack.76.refs_1_, f32[32,1024]{1,0:T(8,128)S(1)} %slice.31.refs_2_, f32[32,1024]{1,0:T(8,128)S(1)} %collective-permute-done.refs_3_, f32[32,1024]{1,0:T(8,128)S(1)} %slice.33.refs_4_, ...), custom_call_target="tpu_custom_call" | custom-call | flops 6442450944 | bytes 4194304 | tf_op jit(solution)/shard_map/pallas_call | solution.py:130
  51.0 2.1 %collective-permute-start.16 = (f32[2,64,512]{2,1,0:T(8,128)S(1)}, f32[2,64,512]{2,1,0:T(8,128)S(1)}, u32[]{:S(2)}, u32[]{:S(2)}) collective-permute-start(f32[2,64,512]{2,1,0:T(8,128)S(1)} %get-tuple-element.39.refs_3_), channel_id=1, source_target_pairs={{1,2},{2,1},{5,6},{6,5},{9,10},{10,9},{13,14},{14,13},{17,18},{18,... | collective-permute-start | bytes 786440 | tf_op jit(solution)/shard_map/ppermute | solution.py:334
  53.1 0.1 collective-permute-start.17
  53.2 5.5 %collective-permute-done.16.refs_5_ = f32[2,64,512]{2,1,0:T(8,128)S(1)} collective-permute-done((f32[2,64,512]{2,1,0:T(8,128)S(1)}, f32[2,64,512]{2,1,0:T(8,128)S(1)}, u32[]{:S(2)}, u32[]{:S(2)}) %collective-permute-start.16) | collective-permute-done | bytes 262176 | tf_op jit(solution)/shard_map/ppermute | solution.py:334
  58.7 0.3 shard_map.61.refs_20_.refs_2_
  59.0 0.7 collective-permute-start.22
  59.7 0.8 collective-permute-start.19
  60.5 1.5 %collective-permute-start.20 = (f32[32,1024]{1,0:T(8,128)S(1)}, f32[32,1024]{1,0:T(8,128)S(1)}, u32[]{:S(2)}, u32[]{:S(2)}) collective-permute-start(f32[32,1024]{1,0:T(8,128)S(1)} %get-tuple-element.55.refs_2_), channel_id=1, source_target_pairs={{0,8},{4,12},{8,16},{12,20},{16,24},{20,28},{24,0},{28,4},{1,9},{5... | collective-permute-start | bytes 393224 | tf_op jit(solution)/shard_map/ppermute | solution.py:289
  62.0 0.8 collective-permute-start.18
  62.8 2.1 %collective-permute-done.22.refs_8_ = f32[32,1024]{1,0:T(8,128)S(1)} collective-permute-done((f32[32,1024]{1,0:T(8,128)S(1)}, f32[32,1024]{1,0:T(8,128)S(1)}, u32[]{:S(2)}, u32[]{:S(2)}) %collective-permute-start.22) | collective-permute-done | bytes 131104 | tf_op jit(solution)/shard_map/ppermute | solution.py:289
  64.9 1.1 %collective-permute-start.26 = (f32[32,1024]{1,0:T(8,128)S(1)}, f32[32,1024]{1,0:T(8,128)S(1)}, u32[]{:S(2)}, u32[]{:S(2)}) collective-permute-start(f32[32,1024]{1,0:T(8,128)S(1)} %collective-permute-done.22.refs_8_), channel_id=1, source_target_pairs={{0,8},{4,12},{8,16},{12,20},{16,24},{20,28},{24,0},{28,4},{1,9},{5... | collective-permute-start | bytes 393224 | tf_op jit(solution)/shard_map/ppermute | solution.py:289
  66.0 1.2 %collective-permute-start.23 = (f32[32,1024]{1,0:T(8,128)S(1)}, f32[32,1024]{1,0:T(8,128)S(1)}, u32[]{:S(2)}, u32[]{:S(2)}) collective-permute-start(f32[32,1024]{1,0:T(8,128)S(1)} %collective-permute-done.22.refs_8_), channel_id=1, source_target_pairs={{0,4},{4,0},{8,12},{12,8},{16,20},{20,16},{24,28},{28,24},{1,5},{5... | collective-permute-start | bytes 393224 | tf_op jit(solution)/shard_map/ppermute | solution.py:286
  67.3 0.2 collective-permute-start.24
  67.5 2.1 %collective-permute-start.21 = (f32[32,1024]{1,0:T(8,128)S(1)}, f32[32,1024]{1,0:T(8,128)S(1)}, u32[]{:S(2)}, u32[]{:S(2)}) collective-permute-start(f32[32,1024]{1,0:T(8,128)S(1)} %collective-permute-done.20.refs_6_), channel_id=1, source_target_pairs={{0,4},{4,0},{8,12},{12,8},{16,20},{20,16},{24,28},{28,24},{1,5},{5... | collective-permute-start | bytes 393224 | tf_op jit(solution)/shard_map/ppermute | solution.py:286
  69.6 2.6 %collective-permute-done.26.refs_12_ = f32[32,1024]{1,0:T(8,128)S(1)} collective-permute-done((f32[32,1024]{1,0:T(8,128)S(1)}, f32[32,1024]{1,0:T(8,128)S(1)}, u32[]{:S(2)}, u32[]{:S(2)}) %collective-permute-start.26) | collective-permute-done | bytes 131104 | tf_op jit(solution)/shard_map/ppermute | solution.py:289
  72.2 0.3 collective-permute-start.27
  72.5 0.9 collective-permute-done.24.refs_10_
  73.4 0.2 collective-permute-start.28
  73.6 1.0 collective-permute-start.25
  74.6 4.0 %collective-permute-done.30.refs_16_ = f32[32,1024]{1,0:T(8,128)S(1)} collective-permute-done((f32[32,1024]{1,0:T(8,128)S(1)}, f32[32,1024]{1,0:T(8,128)S(1)}, u32[]{:S(2)}, u32[]{:S(2)}) %collective-permute-start.30) | collective-permute-done | bytes 131104 | tf_op jit(solution)/shard_map/ppermute | solution.py:289
  78.6 2.0 %collective-permute-done.28.refs_14_ = f32[32,1024]{1,0:T(8,128)S(1)} collective-permute-done((f32[32,1024]{1,0:T(8,128)S(1)}, f32[32,1024]{1,0:T(8,128)S(1)}, u32[]{:S(2)}, u32[]{:S(2)}) %collective-permute-start.28) | collective-permute-done | bytes 131104 | tf_op jit(solution)/shard_map/ppermute | solution.py:289
  80.7 0.6 collective-permute-start.29
  81.3 1.2 %collective-permute-done.31.refs_17_ = f32[32,1024]{1,0:T(8,128)S(1)} collective-permute-done((f32[32,1024]{1,0:T(8,128)S(1)}, f32[32,1024]{1,0:T(8,128)S(1)}, u32[]{:S(2)}, u32[]{:S(2)}) %collective-permute-start.31) | collective-permute-done | bytes 131104 | tf_op jit(solution)/shard_map/ppermute | solution.py:286
  82.4 3.1 %collective-permute-done.29.refs_15_ = f32[32,1024]{1,0:T(8,128)S(1)} collective-permute-done((f32[32,1024]{1,0:T(8,128)S(1)}, f32[32,1024]{1,0:T(8,128)S(1)}, u32[]{:S(2)}, u32[]{:S(2)}) %collective-permute-start.29) | collective-permute-done | bytes 131104 | tf_op jit(solution)/shard_map/ppermute | solution.py:286
  85.6 11.5 %shard_map.62 = (f32[64,1024]{1,0:T(8,128)S(1)}, f32[2,64,512]{2,1,0:T(8,128)S(1)}, f32[2,64,512]{2,1,0:T(8,128)S(1)}) custom-call(s32[1]{0:T(128)} %bitcast.refs_0_, s32[16]{0:T(128)S(1)} %stack.76.refs_1_, f32[32,1024]{1,0:T(8,128)S(1)} %get-tuple-element.55.refs_2_, f32[32,1024]{1,0:T(8,128)S(1)} %collective-permute-done.18.refs_3_, ...), custom_call_target="tpu_custom_call" | custom-call | flops 6442450944 | bytes 4194304 | tf_op jit(solution)/shard_map/pallas_call | solution.py:130
  97.0 5.3 %collective-permute-start.32 = (f32[2,64,512]{2,1,0:T(8,128)S(1)}, f32[2,64,512]{2,1,0:T(8,128)S(1)}, u32[]{:S(2)}, u32[]{:S(2)}) collective-permute-start(f32[2,64,512]{2,1,0:T(8,128)S(1)} %get-tuple-element.50.refs_3_), channel_id=1, source_target_pairs={{1,2},{2,1},{5,6},{6,5},{9,10},{10,9},{13,14},{14,13},{17,18},{18,... | collective-permute-start | bytes 786440 | tf_op jit(solution)/shard_map/ppermute | solution.py:334
  102.3 0.1 collective-permute-start.33
  102.4 4.0 %collective-permute-done.32.refs_5_ = f32[2,64,512]{2,1,0:T(8,128)S(1)} collective-permute-done((f32[2,64,512]{2,1,0:T(8,128)S(1)}, f32[2,64,512]{2,1,0:T(8,128)S(1)}, u32[]{:S(2)}, u32[]{:S(2)}) %collective-permute-start.32) | collective-permute-done | bytes 262176 | tf_op jit(solution)/shard_map/ppermute | solution.py:334
  106.4 1.3 %shard_map.63 = (f32[64,8,128]{2,1,0:T(8,128)}, f32[64,8,128]{2,1,0:T(8,128)}) custom-call(s32[1]{0:T(128)} %bitcast.refs_0_, f32[64,1024]{1,0:T(8,128)S(1)} %get-tuple-element.49.refs_1_, f32[64,1024]{1,0:T(8,128)S(1)} %shard_map.61.refs_20_.refs_2_, f32[2,64,512]{2,1,0:T(8,128)S(1)} %get-tuple-element.50.refs_3_, ...), custom_call_target="tpu_custom_call" | custom-call | flops 2621440 | tf_op jit(solution)/shard_map/pallas_call | solution.py:203
  (27 shorter events, 0.1 us)
Async XLA Ops:
  1.7 7.4 %collective-permute-start.2 = (f32[32,1024]{1,0:T(8,128)S(1)}, f32[32,1024]{1,0:T(8,128)S(1)}, u32[]{:S(2)}, u32[]{:S(2)}) collective-permute-start(f32[32,1024]{1,0:T(8,128)S(1)} %slice.31.refs_2_), channel_id=1, source_target_pairs={{0,8},{4,12},{8,16},{12,20},{16,24},{20,28},{24,0},{28,4},{1,9},{5... | collective-permute-start | bytes 393224 | tf_op jit(solution)/shard_map/ppermute | solution.py:289
  3.9 5.3 %collective-permute-start = (f32[32,1024]{1,0:T(8,128)S(1)}, f32[32,1024]{1,0:T(8,128)S(1)}, u32[]{:S(2)}, u32[]{:S(2)}) collective-permute-start(f32[32,1024]{1,0:T(8,128)S(1)} %slice.31.refs_2_), channel_id=1, source_target_pairs={{0,4},{4,0},{8,12},{12,8},{16,20},{20,16},{24,28},{28,24},{1,5},{5... | collective-permute-start | bytes 393224 | tf_op jit(solution)/shard_map/ppermute | solution.py:286
  5.2 5.9 %collective-permute-start.4 = (f32[32,1024]{1,0:T(8,128)S(1)}, f32[32,1024]{1,0:T(8,128)S(1)}, u32[]{:S(2)}, u32[]{:S(2)}) collective-permute-start(f32[32,1024]{1,0:T(8,128)S(1)} %slice.33.refs_4_), channel_id=1, source_target_pairs={{0,8},{4,12},{8,16},{12,20},{16,24},{20,28},{24,0},{28,4},{1,9},{5... | collective-permute-start | bytes 393224 | tf_op jit(solution)/shard_map/ppermute | solution.py:289
  6.5 4.5 %collective-permute-start.1 = (f32[32,1024]{1,0:T(8,128)S(1)}, f32[32,1024]{1,0:T(8,128)S(1)}, u32[]{:S(2)}, u32[]{:S(2)}) collective-permute-start(f32[32,1024]{1,0:T(8,128)S(1)} %slice.33.refs_4_), channel_id=1, source_target_pairs={{0,4},{4,0},{8,12},{12,8},{16,20},{20,16},{24,28},{28,24},{1,5},{5... | collective-permute-start | bytes 393224 | tf_op jit(solution)/shard_map/ppermute | solution.py:286
  9.1 5.6 %collective-permute-start.6 = (f32[32,1024]{1,0:T(8,128)S(1)}, f32[32,1024]{1,0:T(8,128)S(1)}, u32[]{:S(2)}, u32[]{:S(2)}) collective-permute-start(f32[32,1024]{1,0:T(8,128)S(1)} %collective-permute-done.2.refs_6_), channel_id=1, source_target_pairs={{0,8},{4,12},{8,16},{12,20},{16,24},{20,28},{24,0},{28,4},{1,9},{5... | collective-permute-start | bytes 393224 | tf_op jit(solution)/shard_map/ppermute | solution.py:289
  9.3 5.4 %collective-permute-start.3 = (f32[32,1024]{1,0:T(8,128)S(1)}, f32[32,1024]{1,0:T(8,128)S(1)}, u32[]{:S(2)}, u32[]{:S(2)}) collective-permute-start(f32[32,1024]{1,0:T(8,128)S(1)} %collective-permute-done.2.refs_6_), channel_id=1, source_target_pairs={{0,4},{4,0},{8,12},{12,8},{16,20},{20,16},{24,28},{28,24},{1,5},{5... | collective-permute-start | bytes 393224 | tf_op jit(solution)/shard_map/ppermute | solution.py:286
  11.1 7.1 %collective-permute-start.8 = (f32[32,1024]{1,0:T(8,128)S(1)}, f32[32,1024]{1,0:T(8,128)S(1)}, u32[]{:S(2)}, u32[]{:S(2)}) collective-permute-start(f32[32,1024]{1,0:T(8,128)S(1)} %collective-permute-done.4.refs_8_), channel_id=1, source_target_pairs={{0,8},{4,12},{8,16},{12,20},{16,24},{20,28},{24,0},{28,4},{1,9},{5... | collective-permute-start | bytes 393224 | tf_op jit(solution)/shard_map/ppermute | solution.py:289
  12.1 6.1 %collective-permute-start.5 = (f32[32,1024]{1,0:T(8,128)S(1)}, f32[32,1024]{1,0:T(8,128)S(1)}, u32[]{:S(2)}, u32[]{:S(2)}) collective-permute-start(f32[32,1024]{1,0:T(8,128)S(1)} %collective-permute-done.4.refs_8_), channel_id=1, source_target_pairs={{0,4},{4,0},{8,12},{12,8},{16,20},{20,16},{24,28},{28,24},{1,5},{5... | collective-permute-start | bytes 393224 | tf_op jit(solution)/shard_map/ppermute | solution.py:286
  14.7 13.5 %collective-permute-start.10 = (f32[32,1024]{1,0:T(8,128)S(1)}, f32[32,1024]{1,0:T(8,128)S(1)}, u32[]{:S(2)}, u32[]{:S(2)}) collective-permute-start(f32[32,1024]{1,0:T(8,128)S(1)} %collective-permute-done.6.refs_10_), channel_id=1, source_target_pairs={{0,8},{4,12},{8,16},{12,20},{16,24},{20,28},{24,0},{28,4},{1,9},{5... | collective-permute-start | bytes 393224 | tf_op jit(solution)/shard_map/ppermute | solution.py:289
  15.5 12.7 %collective-permute-start.7 = (f32[32,1024]{1,0:T(8,128)S(1)}, f32[32,1024]{1,0:T(8,128)S(1)}, u32[]{:S(2)}, u32[]{:S(2)}) collective-permute-start(f32[32,1024]{1,0:T(8,128)S(1)} %collective-permute-done.6.refs_10_), channel_id=1, source_target_pairs={{0,4},{4,0},{8,12},{12,8},{16,20},{20,16},{24,28},{28,24},{1,5},{5... | collective-permute-start | bytes 393224 | tf_op jit(solution)/shard_map/ppermute | solution.py:286
  18.2 10.1 %collective-permute-start.12 = (f32[32,1024]{1,0:T(8,128)S(1)}, f32[32,1024]{1,0:T(8,128)S(1)}, u32[]{:S(2)}, u32[]{:S(2)}) collective-permute-start(f32[32,1024]{1,0:T(8,128)S(1)} %collective-permute-done.8.refs_12_), channel_id=1, source_target_pairs={{0,8},{4,12},{8,16},{12,20},{16,24},{20,28},{24,0},{28,4},{1,9},{5... | collective-permute-start | bytes 393224 | tf_op jit(solution)/shard_map/ppermute | solution.py:289
  18.2 10.1 %collective-permute-start.9 = (f32[32,1024]{1,0:T(8,128)S(1)}, f32[32,1024]{1,0:T(8,128)S(1)}, u32[]{:S(2)}, u32[]{:S(2)}) collective-permute-start(f32[32,1024]{1,0:T(8,128)S(1)} %collective-permute-done.8.refs_12_), channel_id=1, source_target_pairs={{0,4},{4,0},{8,12},{12,8},{16,20},{20,16},{24,28},{28,24},{1,5},{5... | collective-permute-start | bytes 393224 | tf_op jit(solution)/shard_map/ppermute | solution.py:286
  20.8 12.7 %collective-permute-start.14 = (f32[33,4,128]{2,1,0:T(4,128)S(1)}, f32[33,4,128]{2,1,0:T(4,128)S(1)}, u32[]{:S(2)}, u32[]{:S(2)}) collective-permute-start(f32[33,4,128]{2,1,0:T(4,128)S(1)} %pad_maximum_fusion), channel_id=1, source_target_pairs={{0,1},{1,2},{2,3},{4,5},{5,6},{6,7},{8,9},{9,10},{10,11},{12,13},{... | collective-permute-start | bytes 202760 | tf_op jit(solution)/shard_map/ppermute | solution.py:320
  28.2 9.1 %collective-permute-start.11 = (f32[32,1024]{1,0:T(8,128)S(1)}, f32[32,1024]{1,0:T(8,128)S(1)}, u32[]{:S(2)}, u32[]{:S(2)}) collective-permute-start(f32[32,1024]{1,0:T(8,128)S(1)} %collective-permute-done.10.refs_14_), channel_id=1, source_target_pairs={{0,4},{4,0},{8,12},{12,8},{16,20},{20,16},{24,28},{28,24},{1,5},{5... | collective-permute-start | bytes 393224 | tf_op jit(solution)/shard_map/ppermute | solution.py:286
  28.3 9.0 %collective-permute-start.13 = (f32[32,1024]{1,0:T(8,128)S(1)}, f32[32,1024]{1,0:T(8,128)S(1)}, u32[]{:S(2)}, u32[]{:S(2)}) collective-permute-start(f32[32,1024]{1,0:T(8,128)S(1)} %collective-permute-done.12.refs_16_), channel_id=1, source_target_pairs={{0,4},{4,0},{8,12},{12,8},{16,20},{20,16},{24,28},{28,24},{1,5},{5... | collective-permute-start | bytes 393224 | tf_op jit(solution)/shard_map/ppermute | solution.py:286
  29.8 5.6 %collective-permute-start.15 = (f32[33,4,128]{2,1,0:T(4,128)S(1)}, f32[33,4,128]{2,1,0:T(4,128)S(1)}, u32[]{:S(2)}, u32[]{:S(2)}) collective-permute-start(f32[33,4,128]{2,1,0:T(4,128)S(1)} %pad_maximum_fusion.1), channel_id=1, source_target_pairs={{1,0},{2,1},{3,2},{5,4},{6,5},{7,6},{9,8},{10,9},{11,10},{13,12},{... | collective-permute-start | bytes 202760 | tf_op jit(solution)/shard_map/ppermute | solution.py:321
  35.4 0.9 copy-start
  37.3 2.2 %copy-start.1 = (f32[32,64,512]{2,1,0:T(8,128)S(1)}, f32[32,64,512]{2,1,0:T(8,128)}, u32[]{:S(2)}) copy-start(f32[32,64,512]{2,1,0:T(8,128)} %refs_18_.3) | copy-start | bytes 12582916
  39.5 46.0 %copy-start.2 = (f32[32,64,512]{2,1,0:T(8,128)S(1)}, f32[32,64,512]{2,1,0:T(8,128)}, u32[]{:S(2)}) copy-start(f32[32,64,512]{2,1,0:T(8,128)} %refs_18_.3) | copy-start | bytes 12582916
  51.0 7.7 %collective-permute-start.16 = (f32[2,64,512]{2,1,0:T(8,128)S(1)}, f32[2,64,512]{2,1,0:T(8,128)S(1)}, u32[]{:S(2)}, u32[]{:S(2)}) collective-permute-start(f32[2,64,512]{2,1,0:T(8,128)S(1)} %get-tuple-element.39.refs_3_), channel_id=1, source_target_pairs={{1,2},{2,1},{5,6},{6,5},{9,10},{10,9},{13,14},{14,13},{17,18},{18,... | collective-permute-start | bytes 786440 | tf_op jit(solution)/shard_map/ppermute | solution.py:334
  53.1 5.6 %collective-permute-start.17 = (f32[2,64,512]{2,1,0:T(8,128)S(1)}, f32[2,64,512]{2,1,0:T(8,128)S(1)}, u32[]{:S(2)}, u32[]{:S(2)}) collective-permute-start(f32[2,64,512]{2,1,0:T(8,128)S(1)} %get-tuple-element.40.refs_4_), channel_id=1, source_target_pairs={{0,1},{2,3},{1,0},{3,2},{4,5},{6,7},{5,4},{7,6},{8,9},{10,11},{9,8... | collective-permute-start | bytes 786440 | tf_op jit(solution)/shard_map/ppermute | solution.py:335
  59.0 5.9 %collective-permute-start.22 = (f32[32,1024]{1,0:T(8,128)S(1)}, f32[32,1024]{1,0:T(8,128)S(1)}, u32[]{:S(2)}, u32[]{:S(2)}) collective-permute-start(f32[32,1024]{1,0:T(8,128)S(1)} %get-tuple-element.54.refs_4_), channel_id=1, source_target_pairs={{0,8},{4,12},{8,16},{12,20},{16,24},{20,28},{24,0},{28,4},{1,9},{5... | collective-permute-start | bytes 393224 | tf_op jit(solution)/shard_map/ppermute | solution.py:289
  59.7 5.2 %collective-permute-start.19 = (f32[32,1024]{1,0:T(8,128)S(1)}, f32[32,1024]{1,0:T(8,128)S(1)}, u32[]{:S(2)}, u32[]{:S(2)}) collective-permute-start(f32[32,1024]{1,0:T(8,128)S(1)} %get-tuple-element.54.refs_4_), channel_id=1, source_target_pairs={{0,4},{4,0},{8,12},{12,8},{16,20},{20,16},{24,28},{28,24},{1,5},{5... | collective-permute-start | bytes 393224 | tf_op jit(solution)/shard_map/ppermute | solution.py:286
  60.5 6.8 %collective-permute-start.20 = (f32[32,1024]{1,0:T(8,128)S(1)}, f32[32,1024]{1,0:T(8,128)S(1)}, u32[]{:S(2)}, u32[]{:S(2)}) collective-permute-start(f32[32,1024]{1,0:T(8,128)S(1)} %get-tuple-element.55.refs_2_), channel_id=1, source_target_pairs={{0,8},{4,12},{8,16},{12,20},{16,24},{20,28},{24,0},{28,4},{1,9},{5... | collective-permute-start | bytes 393224 | tf_op jit(solution)/shard_map/ppermute | solution.py:289
  62.0 5.3 %collective-permute-start.18 = (f32[32,1024]{1,0:T(8,128)S(1)}, f32[32,1024]{1,0:T(8,128)S(1)}, u32[]{:S(2)}, u32[]{:S(2)}) collective-permute-start(f32[32,1024]{1,0:T(8,128)S(1)} %get-tuple-element.55.refs_2_), channel_id=1, source_target_pairs={{0,4},{4,0},{8,12},{12,8},{16,20},{20,16},{24,28},{28,24},{1,5},{5... | collective-permute-start | bytes 393224 | tf_op jit(solution)/shard_map/ppermute | solution.py:286
  64.9 7.3 %collective-permute-start.26 = (f32[32,1024]{1,0:T(8,128)S(1)}, f32[32,1024]{1,0:T(8,128)S(1)}, u32[]{:S(2)}, u32[]{:S(2)}) collective-permute-start(f32[32,1024]{1,0:T(8,128)S(1)} %collective-permute-done.22.refs_8_), channel_id=1, source_target_pairs={{0,8},{4,12},{8,16},{12,20},{16,24},{20,28},{24,0},{28,4},{1,9},{5... | collective-permute-start | bytes 393224 | tf_op jit(solution)/shard_map/ppermute | solution.py:289
  66.0 6.2 %collective-permute-start.23 = (f32[32,1024]{1,0:T(8,128)S(1)}, f32[32,1024]{1,0:T(8,128)S(1)}, u32[]{:S(2)}, u32[]{:S(2)}) collective-permute-start(f32[32,1024]{1,0:T(8,128)S(1)} %collective-permute-done.22.refs_8_), channel_id=1, source_target_pairs={{0,4},{4,0},{8,12},{12,8},{16,20},{20,16},{24,28},{28,24},{1,5},{5... | collective-permute-start | bytes 393224 | tf_op jit(solution)/shard_map/ppermute | solution.py:286
  67.3 6.1 %collective-permute-start.24 = (f32[32,1024]{1,0:T(8,128)S(1)}, f32[32,1024]{1,0:T(8,128)S(1)}, u32[]{:S(2)}, u32[]{:S(2)}) collective-permute-start(f32[32,1024]{1,0:T(8,128)S(1)} %collective-permute-done.20.refs_6_), channel_id=1, source_target_pairs={{0,8},{4,12},{8,16},{12,20},{16,24},{20,28},{24,0},{28,4},{1,9},{5... | collective-permute-start | bytes 393224 | tf_op jit(solution)/shard_map/ppermute | solution.py:289
  67.5 5.9 %collective-permute-start.21 = (f32[32,1024]{1,0:T(8,128)S(1)}, f32[32,1024]{1,0:T(8,128)S(1)}, u32[]{:S(2)}, u32[]{:S(2)}) collective-permute-start(f32[32,1024]{1,0:T(8,128)S(1)} %collective-permute-done.20.refs_6_), channel_id=1, source_target_pairs={{0,4},{4,0},{8,12},{12,8},{16,20},{20,16},{24,28},{28,24},{1,5},{5... | collective-permute-start | bytes 393224 | tf_op jit(solution)/shard_map/ppermute | solution.py:286
  72.2 6.4 %collective-permute-start.30 = (f32[32,1024]{1,0:T(8,128)S(1)}, f32[32,1024]{1,0:T(8,128)S(1)}, u32[]{:S(2)}, u32[]{:S(2)}) collective-permute-start(f32[32,1024]{1,0:T(8,128)S(1)} %collective-permute-done.26.refs_12_), channel_id=1, source_target_pairs={{0,8},{4,12},{8,16},{12,20},{16,24},{20,28},{24,0},{28,4},{1,9},{5... | collective-permute-start | bytes 393224 | tf_op jit(solution)/shard_map/ppermute | solution.py:289
  72.2 6.4 %collective-permute-start.27 = (f32[32,1024]{1,0:T(8,128)S(1)}, f32[32,1024]{1,0:T(8,128)S(1)}, u32[]{:S(2)}, u32[]{:S(2)}) collective-permute-start(f32[32,1024]{1,0:T(8,128)S(1)} %collective-permute-done.26.refs_12_), channel_id=1, source_target_pairs={{0,4},{4,0},{8,12},{12,8},{16,20},{20,16},{24,28},{28,24},{1,5},{5... | collective-permute-start | bytes 393224 | tf_op jit(solution)/shard_map/ppermute | solution.py:286
  73.4 7.3 %collective-permute-start.28 = (f32[32,1024]{1,0:T(8,128)S(1)}, f32[32,1024]{1,0:T(8,128)S(1)}, u32[]{:S(2)}, u32[]{:S(2)}) collective-permute-start(f32[32,1024]{1,0:T(8,128)S(1)} %collective-permute-done.24.refs_10_), channel_id=1, source_target_pairs={{0,8},{4,12},{8,16},{12,20},{16,24},{20,28},{24,0},{28,4},{1,9},{5... | collective-permute-start | bytes 393224 | tf_op jit(solution)/shard_map/ppermute | solution.py:289
  73.6 7.0 %collective-permute-start.25 = (f32[32,1024]{1,0:T(8,128)S(1)}, f32[32,1024]{1,0:T(8,128)S(1)}, u32[]{:S(2)}, u32[]{:S(2)}) collective-permute-start(f32[32,1024]{1,0:T(8,128)S(1)} %collective-permute-done.24.refs_10_), channel_id=1, source_target_pairs={{0,4},{4,0},{8,12},{12,8},{16,20},{20,16},{24,28},{28,24},{1,5},{5... | collective-permute-start | bytes 393224 | tf_op jit(solution)/shard_map/ppermute | solution.py:286
  78.6 3.8 %collective-permute-start.31 = (f32[32,1024]{1,0:T(8,128)S(1)}, f32[32,1024]{1,0:T(8,128)S(1)}, u32[]{:S(2)}, u32[]{:S(2)}) collective-permute-start(f32[32,1024]{1,0:T(8,128)S(1)} %collective-permute-done.30.refs_16_), channel_id=1, source_target_pairs={{0,4},{4,0},{8,12},{12,8},{16,20},{20,16},{24,28},{28,24},{1,5},{5... | collective-permute-start | bytes 393224 | tf_op jit(solution)/shard_map/ppermute | solution.py:286
  80.7 4.9 %collective-permute-start.29 = (f32[32,1024]{1,0:T(8,128)S(1)}, f32[32,1024]{1,0:T(8,128)S(1)}, u32[]{:S(2)}, u32[]{:S(2)}) collective-permute-start(f32[32,1024]{1,0:T(8,128)S(1)} %collective-permute-done.28.refs_14_), channel_id=1, source_target_pairs={{0,4},{4,0},{8,12},{12,8},{16,20},{20,16},{24,28},{28,24},{1,5},{5... | collective-permute-start | bytes 393224 | tf_op jit(solution)/shard_map/ppermute | solution.py:286
  97.0 9.3 %collective-permute-start.32 = (f32[2,64,512]{2,1,0:T(8,128)S(1)}, f32[2,64,512]{2,1,0:T(8,128)S(1)}, u32[]{:S(2)}, u32[]{:S(2)}) collective-permute-start(f32[2,64,512]{2,1,0:T(8,128)S(1)} %get-tuple-element.50.refs_3_), channel_id=1, source_target_pairs={{1,2},{2,1},{5,6},{6,5},{9,10},{10,9},{13,14},{14,13},{17,18},{18,... | collective-permute-start | bytes 786440 | tf_op jit(solution)/shard_map/ppermute | solution.py:334
  102.3 4.0 %collective-permute-start.33 = (f32[2,64,512]{2,1,0:T(8,128)S(1)}, f32[2,64,512]{2,1,0:T(8,128)S(1)}, u32[]{:S(2)}, u32[]{:S(2)}) collective-permute-start(f32[2,64,512]{2,1,0:T(8,128)S(1)} %get-tuple-element.51.refs_4_), channel_id=1, source_target_pairs={{0,1},{2,3},{1,0},{3,2},{4,5},{6,7},{5,4},{7,6},{8,9},{10,11},{9,8... | collective-permute-start | bytes 786440 | tf_op jit(solution)/shard_map/ppermute | solution.py:335
